TPU v7x, 32 devices: a whole 2x2x4 slice. The times are simulated.
32 devices in a mesh: member: 4 (over y, x), tile: 8 (over z, core).
Axes of the slice: x: 2, y: 2, z: 4, core: 2. Of those that a mesh axis runs over, the one named last changes fastest.
Arguments:
- density: float32 [4, 6, 128, 128], P('member', None, 'tile'), may hold values from 0.05 to 5
- scaling: float32 [4, 6, 128, 128], P('member', None, 'tile'), may hold values from 0.2 to 5
- member_weights: float32 [4], P('member'), may hold values from 0.5 to 11
- seams: int32 [3, 4, 6], replicated, may hold values from 0 to 5, as said below
Outputs:
- new_scaling: float32 [4, 6, 128, 128], P('member', None, 'tile')
- dual_scaling: float32 [4, 6, 128, 128], P('member', None, 'tile')
- barycenter: float32 [6, 128, 128], P(None, 'tile')
Inputs may be any that keep to these rules, and one draw needn't show every extreme that they name: Edges are numbered 0 first row, 1 last row, 2 first column, 3 last column. The table describes the six faces of a cube, each face's frame turned or mirrored: seams[0, e, f] is the face across edge e of face f, seams[1, e, f] the edge of that face which meets it, and the relation is symmetric; seams[2, e, f] is 1 where positions along the seam run opposite ways on the two faces, and the same from both sides.
All inputs are finite; a program needn't handle non-finite values.
Results may differ from a plain program's by a relative error of at most 0.00007.
Values sent between devices are 32-bit elements; how exact they have to be, the bound alone decides.
A program may use at most 64 MiB of HBM per device.

v0:
```python
import jax
import jax.numpy as jnp
from jax import lax
from jax.sharding import PartitionSpec as P

STEPS = 4


KAPPA = 0.24


def with_halo(block, sides, width):
    for axis, dim in sides:
        count = lax.axis_size(axis)
        forward = [(i, i + 1) for i in range(count - 1)]
        backward = [(target, source) for source, target in forward]
        low = lax.ppermute(
            lax.slice_in_dim(block, block.shape[dim] - width, None, axis=dim), axis, forward
        )
        high = lax.ppermute(lax.slice_in_dim(block, 0, width, axis=dim), axis, backward)
        block = jnp.concatenate([low, block, high], axis=dim)
    return block


def body(density, scaling, member_weights, seams):
    tiles = lax.axis_size("tile")
    position = lax.axis_index("tile")
    members = scaling.shape[0]
    faces = scaling.shape[1]
    rows = scaling.shape[2]
    side = scaling.shape[3]
    is_first = (position == 0).astype(jnp.float32)
    is_last = (position == tiles - 1).astype(jnp.float32)
    slots = jnp.arange(4 * faces, dtype=jnp.int32)
    selectors = []
    for edge_id in range(4):
        wanted = seams[0, edge_id] * 4 + seams[1, edge_id]
        selectors.append((wanted[:, None] == slots[None, :]).astype(jnp.float32))

    def edge_table(field):
        first_row = field[:, :, 0, :] * is_first
        last_row = field[:, :, -1, :] * is_last
        empty = jnp.zeros((members, faces, 2, side), jnp.float32)
        column_pieces = jnp.stack([field[:, :, :, 0], field[:, :, :, -1]], axis=2)
        placed = lax.dynamic_update_slice_in_dim(empty, column_pieces, position * rows, 3)
        local = jnp.concatenate([jnp.stack([first_row, last_row], axis=2), placed], axis=2)
        return lax.psum(local, "tile")

    def ghost(table, edge_id):
        flat = table.reshape(members, faces * 4, side)
        taken = jnp.einsum("fq,mqn->mfn", selectors[edge_id], flat, precision=lax.Precision.HIGHEST)
        return jnp.where((seams[2, edge_id] == 1)[None, :, None], taken[..., ::-1], taken)

    def diffuse(field):
        widened = with_halo(field, (("tile", 2),), 1)
        table = edge_table(field)
        upper = ghost(table, 0)
        lower = ghost(table, 1)
        start = position * rows
        left = lax.dynamic_slice_in_dim(ghost(table, 2), start, rows, 2)
        right = lax.dynamic_slice_in_dim(ghost(table, 3), start, rows, 2)
        top_row = jnp.where(position == 0, upper, widened[:, :, 0, :])
        bottom_row = jnp.where(position == tiles - 1, lower, widened[:, :, -1, :])
        widened = jnp.concatenate(
            [top_row[:, :, None, :], field, bottom_row[:, :, None, :]], axis=2
        )
        vertical = widened[:, :, :-2, :] + widened[:, :, 2:, :]
        lateral = jnp.concatenate([left[..., None], field[..., :-1]], axis=3) + jnp.concatenate(
            [field[..., 1:], right[..., None]], axis=3
        )
        return field + KAPPA * (vertical + lateral - 4.0 * field)

    def kernel(field):
        for counter in range(STEPS):
            field = diffuse(field)
        return field

    dual_scaling = density / kernel(scaling)
    marginal = scaling * kernel(dual_scaling)
    log_marginal = jnp.log(marginal)
    weighted = jnp.einsum(
        "k,kfrc->frc", member_weights, log_marginal, precision=lax.Precision.HIGHEST
    )
    weight_local = jnp.sum(member_weights)
    summed, weight_sum = lax.psum((weighted, weight_local), "member")
    barycenter = jnp.exp(summed / weight_sum)
    new_scaling = scaling * barycenter[None] / marginal
    return (new_scaling, dual_scaling, barycenter)


def solution(mesh):
    return jax.shard_map(
        body,
        mesh=mesh,
        in_specs=(
            P("member", None, "tile", None),
            P("member", None, "tile", None),
            P("member"),
            P(),
        ),
        out_specs=(
            P("member", None, "tile", None),
            P("member", None, "tile", None),
            P(None, "tile", None),
        ),
        check_vma=False,
    )
```

profile of v0, /device:TPU:0, one launch (start us, length us, event | category | flops | bytes accessed | tf_op | source)
XLA Modules:
  0.0 292.6 jit_solution(8402390046479961587)
XLA Ops:
  0.7 0.9 copy.123
  1.6 2.4 collective-permute-start
  3.9 1.3 collective-permute-start.1
  5.6 0.2 dynamic_update_slice.24
  5.8 32.0 %psum.70 = f32[24,128]{1,0:T(8,128)S(1)} all-reduce(f32[24,128]{1,0:T(8,128)S(1)} %bitcast.302), channel_id=1, replica_groups=mesh['member'=4,'tile'=8] {'tile'}, use_global_device_ids=true, to_apply=%region_0.0 | all-reduce | flops 3072 | bytes 24576 | tf_op jit(solution)/shard_map/psum | solution.py:47
  38.2 0.2 convolution_bitcast_fusion.30
  38.4 0.2 convolution_bitcast_fusion.31
  40.8 0.2 dynamic_update_slice.25
  41.0 26.0 %psum.71 = f32[24,128]{1,0:T(8,128)S(1)} all-reduce(f32[24,128]{1,0:T(8,128)S(1)} %bitcast.303), channel_id=1, replica_groups=mesh['member'=4,'tile'=8] {'tile'}, use_global_device_ids=true, to_apply=%region_1.2 | all-reduce | flops 3072 | bytes 24576 | tf_op jit(solution)/shard_map/psum | solution.py:47
  67.8 1.3 collective-permute-start.2
  69.1 1.3 collective-permute-start.3
  71.4 0.8 collective-permute-done.3
  72.8 0.2 dynamic_update_slice.26
  73.1 27.1 %psum.72 = f32[24,128]{1,0:T(8,128)S(1)} all-reduce(f32[24,128]{1,0:T(8,128)S(1)} %bitcast.304), channel_id=1, replica_groups=mesh['member'=4,'tile'=8] {'tile'}, use_global_device_ids=true, to_apply=%region_2.3 | all-reduce | flops 3072 | bytes 24576 | tf_op jit(solution)/shard_map/psum | solution.py:47
  101.0 1.3 collective-permute-start.4
  102.3 1.3 collective-permute-start.5
  104.5 0.8 collective-permute-done.5
  106.0 0.2 dynamic_update_slice.27
  106.2 27.1 %psum.73 = f32[24,128]{1,0:T(8,128)S(1)} all-reduce(f32[24,128]{1,0:T(8,128)S(1)} %bitcast.305), channel_id=1, replica_groups=mesh['member'=4,'tile'=8] {'tile'}, use_global_device_ids=true, to_apply=%region_3.4 | all-reduce | flops 3072 | bytes 24576 | tf_op jit(solution)/shard_map/psum | solution.py:47
  133.9 0.2 convolution_bitcast_fusion.19
  134.1 1.3 collective-permute-start.6
  135.4 1.3 collective-permute-start.7
  137.7 0.8 collective-permute-done.7
  138.7 0.6 copy.125
  139.8 0.2 dynamic_update_slice.28
  140.0 27.5 %psum.74 = f32[24,128]{1,0:T(8,128)S(1)} all-reduce(f32[24,128]{1,0:T(8,128)S(1)} %bitcast.306), channel_id=1, replica_groups=mesh['member'=4,'tile'=8] {'tile'}, use_global_device_ids=true, to_apply=%region_4.5 | all-reduce | flops 3072 | bytes 24576 | tf_op jit(solution)/shard_map/psum | solution.py:47
  168.2 1.3 collective-permute-start.8
  169.5 1.3 collective-permute-start.9
  171.8 0.8 collective-permute-done.9
  173.2 0.2 dynamic_update_slice.29
  173.5 27.1 %psum.75 = f32[24,128]{1,0:T(8,128)S(1)} all-reduce(f32[24,128]{1,0:T(8,128)S(1)} %bitcast.307), channel_id=1, replica_groups=mesh['member'=4,'tile'=8] {'tile'}, use_global_device_ids=true, to_apply=%region_5.6 | all-reduce | flops 3072 | bytes 24576 | tf_op jit(solution)/shard_map/psum | solution.py:47
  201.4 1.3 collective-permute-start.10
  202.7 1.3 collective-permute-start.11
  204.9 0.8 collective-permute-done.11
  206.4 0.2 dynamic_update_slice.30
  206.6 27.1 %psum.76 = f32[24,128]{1,0:T(8,128)S(1)} all-reduce(f32[24,128]{1,0:T(8,128)S(1)} %bitcast.308), channel_id=1, replica_groups=mesh['member'=4,'tile'=8] {'tile'}, use_global_device_ids=true, to_apply=%region_6.7 | all-reduce | flops 3072 | bytes 24576 | tf_op jit(solution)/shard_map/psum | solution.py:47
  234.5 1.3 collective-permute-start.12
  235.8 1.3 collective-permute-start.13
  238.0 0.8 collective-permute-done.13
  239.5 0.2 dynamic_update_slice.31
  239.8 27.1 %psum.77 = f32[24,128]{1,0:T(8,128)S(1)} all-reduce(f32[24,128]{1,0:T(8,128)S(1)} %bitcast.309), channel_id=1, replica_groups=mesh['member'=4,'tile'=8] {'tile'}, use_global_device_ids=true, to_apply=%region_7.8 | all-reduce | flops 3072 | bytes 24576 | tf_op jit(solution)/shard_map/psum | solution.py:47
  267.7 1.3 collective-permute-start.14
  269.0 1.3 collective-permute-start.15
  271.1 0.9 collective-permute-done.15
  272.2 18.5 %all-reduce = (f32[6,16,128]{2,0,1:T(8,128)S(1)}, f32[]{:T(128)}) all-reduce(f32[6,16,128]{2,0,1:T(8,128)S(1)} %get-tuple-element.15, f32[]{:T(128)} %bitcast.126), channel_id=1, replica_groups=mesh['member'=4,'tile'=8] {'member'}, use_global_device_ids=true, to_apply=%region_8.9 | all-reduce | flops 12289 | bytes 98312 | tf_op jit(solution)/shard_map/psum | solution.py:85
  290.7 0.7 fusion.42
  291.4 0.6 copy.124
  292.0 0.6 copy.126
  (245 shorter events, 17.5 us)
Async XLA Ops:
  0.6 4.6 %copy-start = (f32[1,6,16,128]{3,2,1,0:T(8,128)S(1)}, f32[1,6,16,128]{3,2,1,0:T(8,128)}, u32[]{:S(2)}) copy-start(f32[1,6,16,128]{3,2,1,0:T(8,128)} %param.5) | copy-start | bytes 147460
  1.5 3.7 %copy-start.2 = (s32[3,4,6]{2,1,0:T(4,128)S(1)}, s32[3,4,6]{2,1,0:T(4,128)}, u32[]{:S(2)}) copy-start(s32[3,4,6]{2,1,0:T(4,128)} %param.7) | copy-start | bytes 868
  1.6 38.5 %collective-permute-start = (f32[1,6,1,128]{3,1,2,0:T(8,128)S(1)}, f32[1,6,1,128]{3,1,2,0:T(8,128)S(1)}, u32[]{:S(2)}, u32[]{:S(2)}) collective-permute-start(f32[1,6,1,128]{3,1,2,0:T(8,128)S(1)} %get-tuple-element.75), channel_id=1, source_target_pairs={{0,1},{1,2},{2,3},{3,4},{4,5},{5,6},{6,7},{8,9},{9,10},{10,11},{11... | collective-permute-start | bytes 9224 | tf_op jit(solution)/shard_map/ppermute | solution.py:17
  3.9 36.2 %collective-permute-start.1 = (f32[1,6,1,128]{3,1,2,0:T(8,128)S(1)}, f32[1,6,1,128]{3,1,2,0:T(8,128)S(1)}, u32[]{:S(2)}, u32[]{:S(2)}) collective-permute-start(f32[1,6,1,128]{3,1,2,0:T(8,128)S(1)} %get-tuple-element.78), channel_id=1, source_target_pairs={{1,0},{2,1},{3,2},{4,3},{5,4},{6,5},{7,6},{9,8},{10,9},{11,10},{12... | collective-permute-start | bytes 9224 | tf_op jit(solution)/shard_map/ppermute | solution.py:20
  67.8 3.4 %collective-permute-start.2 = (f32[1,6,1,128]{3,1,2,0:T(8,128)S(1)}, f32[1,6,1,128]{3,1,2,0:T(8,128)S(1)}, u32[]{:S(2)}, u32[]{:S(2)}) collective-permute-start(f32[1,6,1,128]{3,1,2,0:T(8,128)S(1)} %get-tuple-element.67), channel_id=1, source_target_pairs={{0,1},{1,2},{2,3},{3,4},{4,5},{5,6},{6,7},{8,9},{9,10},{10,11},{11... | collective-permute-start | bytes 9224 | tf_op jit(solution)/shard_map/ppermute | solution.py:17
  69.1 3.1 %collective-permute-start.3 = (f32[1,6,1,128]{3,1,2,0:T(8,128)S(1)}, f32[1,6,1,128]{3,1,2,0:T(8,128)S(1)}, u32[]{:S(2)}, u32[]{:S(2)}) collective-permute-start(f32[1,6,1,128]{3,1,2,0:T(8,128)S(1)} %get-tuple-element.70), channel_id=1, source_target_pairs={{1,0},{2,1},{3,2},{4,3},{5,4},{6,5},{7,6},{9,8},{10,9},{11,10},{12... | collective-permute-start | bytes 9224 | tf_op jit(solution)/shard_map/ppermute | solution.py:20
  101.0 3.4 %collective-permute-start.4 = (f32[1,6,1,128]{3,1,2,0:T(8,128)S(1)}, f32[1,6,1,128]{3,1,2,0:T(8,128)S(1)}, u32[]{:S(2)}, u32[]{:S(2)}) collective-permute-start(f32[1,6,1,128]{3,1,2,0:T(8,128)S(1)} %get-tuple-element.59), channel_id=1, source_target_pairs={{0,1},{1,2},{2,3},{3,4},{4,5},{5,6},{6,7},{8,9},{9,10},{10,11},{11... | collective-permute-start | bytes 9224 | tf_op jit(solution)/shard_map/ppermute | solution.py:17
  102.3 3.1 %collective-permute-start.5 = (f32[1,6,1,128]{3,1,2,0:T(8,128)S(1)}, f32[1,6,1,128]{3,1,2,0:T(8,128)S(1)}, u32[]{:S(2)}, u32[]{:S(2)}) collective-permute-start(f32[1,6,1,128]{3,1,2,0:T(8,128)S(1)} %get-tuple-element.62), channel_id=1, source_target_pairs={{1,0},{2,1},{3,2},{4,3},{5,4},{6,5},{7,6},{9,8},{10,9},{11,10},{12... | collective-permute-start | bytes 9224 | tf_op jit(solution)/shard_map/ppermute | solution.py:20
  134.1 3.5 %collective-permute-start.6 = (f32[1,6,1,128]{3,1,2,0:T(8,128)S(1)}, f32[1,6,1,128]{3,1,2,0:T(8,128)S(1)}, u32[]{:S(2)}, u32[]{:S(2)}) collective-permute-start(f32[1,6,1,128]{3,1,2,0:T(8,128)S(1)} %get-tuple-element.51), channel_id=1, source_target_pairs={{0,1},{1,2},{2,3},{3,4},{4,5},{5,6},{6,7},{8,9},{9,10},{10,11},{11... | collective-permute-start | bytes 9224 | tf_op jit(solution)/shard_map/ppermute | solution.py:17
  135.4 3.1 %collective-permute-start.7 = (f32[1,6,1,128]{3,1,2,0:T(8,128)S(1)}, f32[1,6,1,128]{3,1,2,0:T(8,128)S(1)}, u32[]{:S(2)}, u32[]{:S(2)}) collective-permute-start(f32[1,6,1,128]{3,1,2,0:T(8,128)S(1)} %get-tuple-element.54), channel_id=1, source_target_pairs={{1,0},{2,1},{3,2},{4,3},{5,4},{6,5},{7,6},{9,8},{10,9},{11,10},{12... | collective-permute-start | bytes 9224 | tf_op jit(solution)/shard_map/ppermute | solution.py:20
  137.4 1.1 copy-start.1
  168.2 3.4 %collective-permute-start.8 = (f32[1,6,1,128]{3,1,2,0:T(8,128)S(1)}, f32[1,6,1,128]{3,1,2,0:T(8,128)S(1)}, u32[]{:S(2)}, u32[]{:S(2)}) collective-permute-start(f32[1,6,1,128]{3,1,2,0:T(8,128)S(1)} %get-tuple-element.43), channel_id=1, source_target_pairs={{0,1},{1,2},{2,3},{3,4},{4,5},{5,6},{6,7},{8,9},{9,10},{10,11},{11... | collective-permute-start | bytes 9224 | tf_op jit(solution)/shard_map/ppermute | solution.py:17
  169.5 3.1 %collective-permute-start.9 = (f32[1,6,1,128]{3,1,2,0:T(8,128)S(1)}, f32[1,6,1,128]{3,1,2,0:T(8,128)S(1)}, u32[]{:S(2)}, u32[]{:S(2)}) collective-permute-start(f32[1,6,1,128]{3,1,2,0:T(8,128)S(1)} %get-tuple-element.46), channel_id=1, source_target_pairs={{1,0},{2,1},{3,2},{4,3},{5,4},{6,5},{7,6},{9,8},{10,9},{11,10},{12... | collective-permute-start | bytes 9224 | tf_op jit(solution)/shard_map/ppermute | solution.py:20
  201.4 3.4 %collective-permute-start.10 = (f32[1,6,1,128]{3,1,2,0:T(8,128)S(1)}, f32[1,6,1,128]{3,1,2,0:T(8,128)S(1)}, u32[]{:S(2)}, u32[]{:S(2)}) collective-permute-start(f32[1,6,1,128]{3,1,2,0:T(8,128)S(1)} %get-tuple-element.35), channel_id=1, source_target_pairs={{0,1},{1,2},{2,3},{3,4},{4,5},{5,6},{6,7},{8,9},{9,10},{10,11},{11... | collective-permute-start | bytes 9224 | tf_op jit(solution)/shard_map/ppermute | solution.py:17
  202.7 3.1 %collective-permute-start.11 = (f32[1,6,1,128]{3,1,2,0:T(8,128)S(1)}, f32[1,6,1,128]{3,1,2,0:T(8,128)S(1)}, u32[]{:S(2)}, u32[]{:S(2)}) collective-permute-start(f32[1,6,1,128]{3,1,2,0:T(8,128)S(1)} %get-tuple-element.38), channel_id=1, source_target_pairs={{1,0},{2,1},{3,2},{4,3},{5,4},{6,5},{7,6},{9,8},{10,9},{11,10},{12... | collective-permute-start | bytes 9224 | tf_op jit(solution)/shard_map/ppermute | solution.py:20
  234.5 3.4 %collective-permute-start.12 = (f32[1,6,1,128]{3,1,2,0:T(8,128)S(1)}, f32[1,6,1,128]{3,1,2,0:T(8,128)S(1)}, u32[]{:S(2)}, u32[]{:S(2)}) collective-permute-start(f32[1,6,1,128]{3,1,2,0:T(8,128)S(1)} %get-tuple-element.27), channel_id=1, source_target_pairs={{0,1},{1,2},{2,3},{3,4},{4,5},{5,6},{6,7},{8,9},{9,10},{10,11},{11... | collective-permute-start | bytes 9224 | tf_op jit(solution)/shard_map/ppermute | solution.py:17
  235.8 3.1 %collective-permute-start.13 = (f32[1,6,1,128]{3,1,2,0:T(8,128)S(1)}, f32[1,6,1,128]{3,1,2,0:T(8,128)S(1)}, u32[]{:S(2)}, u32[]{:S(2)}) collective-permute-start(f32[1,6,1,128]{3,1,2,0:T(8,128)S(1)} %get-tuple-element.30), channel_id=1, source_target_pairs={{1,0},{2,1},{3,2},{4,3},{5,4},{6,5},{7,6},{9,8},{10,9},{11,10},{12... | collective-permute-start | bytes 9224 | tf_op jit(solution)/shard_map/ppermute | solution.py:20
  267.7 3.4 %collective-permute-start.14 = (f32[1,6,1,128]{3,1,2,0:T(8,128)S(1)}, f32[1,6,1,128]{3,1,2,0:T(8,128)S(1)}, u32[]{:S(2)}, u32[]{:S(2)}) collective-permute-start(f32[1,6,1,128]{3,1,2,0:T(8,128)S(1)} %get-tuple-element.17), channel_id=1, source_target_pairs={{0,1},{1,2},{2,3},{3,4},{4,5},{5,6},{6,7},{8,9},{9,10},{10,11},{11... | collective-permute-start | bytes 9224 | tf_op jit(solution)/shard_map/ppermute | solution.py:17
  269.0 3.1 %collective-permute-start.15 = (f32[1,6,1,128]{3,1,2,0:T(8,128)S(1)}, f32[1,6,1,128]{3,1,2,0:T(8,128)S(1)}, u32[]{:S(2)}, u32[]{:S(2)}) collective-permute-start(f32[1,6,1,128]{3,1,2,0:T(8,128)S(1)} %get-tuple-element.20), channel_id=1, source_target_pairs={{1,0},{2,1},{3,2},{4,3},{5,4},{6,5},{7,6},{9,8},{10,9},{11,10},{12... | collective-permute-start | bytes 9224 | tf_op jit(solution)/shard_map/ppermute | solution.py:20
where the time goes:
time: 293 us
  blocking collectives  240 us (82%)
  starting transfers between devices  21.7 us (7%)
  local copies, waits for them, and re-layouts  12.9 us (4%)
  matrix products  6.02 us (2%)
  waiting for transfers between devices  5.9 us (2%)
  other arithmetic  4.2 us (1%)
    psum x8, blocking collectives, edge_table(): return lax.psum(local, 'tile')  221 us
    psum x1, blocking collectives, body(): summed, weight_sum = lax.psum((weighted, weight_local), 'member')  18.5 us
    ppermute x8, starting transfers between devices, with_halo(): lax.ppermute(lax.slice_in_dim(block, block.shape[dim] - width, None, axis...  11.4 us
    ppermute x8, starting transfers between devices, with_halo(): lax.ppermute(lax.slice_in_dim(block, 0, width, axis=dim), axis, backward)  10.3 us
    dot_general x32, matrix products, ghost(): jnp.einsum('fq,mqn->mfn', selectors[edge_id], flat, precision=lax.Precisi...  6.02 us
    ppermute x8, waiting for transfers between devices, with_halo(): lax.ppermute(lax.slice_in_dim(block, 0, width, axis=dim), axis, backward)  5.88 us
  transfers between devices with their start and end apart: 16, of which 7 were waited for; matrix products, arithmetic and copies ran while one was open for 3% of the time, Pallas kernels for 0%

commit v1 on v0

v1 whole, which is shorter than its diff:
```python
import functools

import jax
import jax.numpy as jnp
from jax import lax
from jax.experimental import pallas as pl
from jax.experimental.pallas import tpu as pltpu
from jax.sharding import PartitionSpec as P

STEPS = 4
KAPPA = 0.24
LANES = 128
MESH = pl.DeviceIdType.MESH


def kernel(
    n, members, faces, rows, side,
    seams_ref, weight_ref, density_ref, scaling_ref,
    new_ref, dual_ref, bary_ref,
    field, dens, pack, packs, top, bottom, first, last, above, below,
    table, columns, ghosts, ghost_columns, logs, others,
    pack_send, pack_recv, top_send, bottom_send, row_recv, log_send, log_recv,
):
    t = lax.axis_index("tile")
    m = lax.axis_index("member")
    groups = faces * rows // 8
    per = LANES // 16
    wide = pl.cdiv(groups, per)
    half = LANES // 8
    narrow = pl.cdiv(groups, half)

    barrier = pltpu.get_barrier_semaphore()
    for i in range(1, n):
        pl.semaphore_signal(barrier, inc=1, device_id={"tile": lax.rem(t + i, n)}, device_id_type=MESH)
    for i in range(1, members):
        pl.semaphore_signal(
            barrier, inc=1, device_id={"member": lax.rem(m + i, members)}, device_id_type=MESH
        )

    lane = lax.broadcasted_iota(jnp.int32, (8, LANES), 1)

    def edge_block(ref, k):
        f, r = (8 * k) // rows, (8 * k) % rows
        low = ref[0, f, r : r + 8, :LANES]
        if side == LANES:
            return low
        return jnp.where(lane < LANES // 2, low, ref[0, f, r : r + 8, side - LANES :])

    for vreg in range(wide):
        out = jnp.ones((8, LANES), jnp.float32)
        for k in range(vreg * per, min(groups, (vreg + 1) * per)):
            at = 16 * (k % per)
            moved = pltpu.roll(edge_block(scaling_ref, k), (8 + at) % LANES, 1)
            out = jnp.where((lane >= at) & (lane < at + 16), moved, out)
        pack[vreg] = out
    for vreg in range(narrow):
        out = jnp.ones((8, LANES), jnp.float32)
        for k in range(vreg * half, min(groups, (vreg + 1) * half)):
            at = 8 * (k % half)
            moved = pltpu.roll(edge_block(density_ref, k), (4 + at) % LANES, 1)
            out = jnp.where((lane >= at) & (lane < at + 8), moved, out)
        pack[wide + vreg] = out
    packs[t] = pack[...]
    top[:faces] = scaling_ref[0, :, :8, :]
    bottom[:faces] = scaling_ref[0, :, rows - 8 :, :]
    for f in range(faces):
        j, s = faces + f // 2, 4 * (f % 2)
        top[j, s : s + 4, :] = density_ref[0, f, :4, :]
        bottom[j, s : s + 4, :] = density_ref[0, f, rows - 4 :, :]

    pl.semaphore_wait(barrier, n - 1 + members - 1)

    def send_pack(peer, slot):
        return pltpu.make_async_remote_copy(
            src_ref=pack, dst_ref=packs.at[slot],
            send_sem=pack_send.at[peer], recv_sem=pack_recv.at[slot],
            device_id={"tile": peer}, device_id_type=MESH,
        )

    def send_rows(src, dst, sems, sem, which, peer):
        return pltpu.make_async_remote_copy(
            src_ref=src, dst_ref=dst, send_sem=sems.at[sem], recv_sem=row_recv.at[which],
            device_id={"tile": peer}, device_id_type=MESH,
        )

    peers = [lax.rem(t + i, n) for i in range(1, n)]
    up_peer = lax.rem(t + n - 1, n)
    down_peer = lax.rem(t + 1, n)
    to_above = send_rows(top, below, top_send, n, 3, up_peer)
    to_below = send_rows(bottom, above, bottom_send, n, 2, down_peer)
    to_first = [send_rows(top, first, top_send, i, 0, peer) for i, peer in enumerate(peers)]
    to_last = [send_rows(bottom, last, bottom_send, i, 1, peer) for i, peer in enumerate(peers)]

    @pl.when(t == 0)
    def _():
        for copy in reversed(to_first):
            copy.start()

    @pl.when(t == n - 1)
    def _():
        for copy in to_last:
            copy.start()

    @pl.when(t > 0)
    def _():
        to_above.start()

    @pl.when(t < n - 1)
    def _():
        to_below.start()

    for peer in peers:
        send_pack(peer, t).start()

    def fill(i, carry):
        at = pl.multiple_of(8 * i, 8)
        for f in range(faces):
            block = jnp.ones((8, side), jnp.float32)
            dens[f, pl.ds(at, 8), :] = block
            field[0, f, pl.ds(at + 8, 8), :] = block
        return carry

    lax.fori_loop(0, side // 8, fill, 0)
    ghosts[...] = jnp.zeros(ghosts.shape, jnp.float32)
    table[...] = jnp.zeros(table.shape, jnp.float32)

    for peer in peers:
        send_pack(peer, peer).wait_recv()

    for s in range(n):
        for k in range(groups):
            f, r = (8 * k) // rows, (8 * k) % rows + rows * s
            value = pltpu.roll(packs[s, k // per], (2 * LANES - 8 - 16 * (k % per)) % LANES, 1)
            field[0, f, 8 + r : 16 + r, :LANES] = value
            other = pltpu.roll(packs[s, wide + k // half], (2 * LANES - 4 - 8 * (k % half)) % LANES, 1)
            dens[f, r : r + 8, :LANES] = other
            if side > LANES:
                field[0, f, 8 + r : 16 + r, side - LANES :] = value
                dens[f, r : r + 8, side - LANES :] = other

    start = pl.multiple_of(rows * t, 8)

    def place(src, at, low):
        at = pl.multiple_of(at, 8) if not isinstance(at, int) else at
        field[0, :, pl.ds(at + 8, 8), :] = src[:faces]
        for f in range(faces):
            j, s = faces + f // 2, 4 * (f % 2)
            four = src[j, s : s + 4, :]
            line_of = lax.broadcasted_iota(jnp.int32, (8, side), 0)
            dens[f, pl.ds(at, 8), :] = jnp.where(
                line_of < 4 if low else line_of >= 4,
                jnp.concatenate([four, four], axis=0),
                dens[f, pl.ds(at, 8), :],
            )

    @pl.when(t > 0)
    def _():
        to_first[0].wait_recv()
        place(first, 0, True)

    @pl.when(t < n - 1)
    def _():
        to_last[0].wait_recv()
        place(last, side - 8, False)

    @pl.when(t > 0)
    def _():
        to_below.wait_recv()
        place(above, start - 8, False)

    @pl.when(t < n - 1)
    def _():
        to_above.wait_recv()
        place(below, start + rows, True)

    field[0, :, pl.ds(start + 8, rows), :] = scaling_ref[0]
    dens[:, pl.ds(start, rows), :] = density_ref[0]

    slots = []
    for e in range(4):
        slots.append([])
        for f in range(faces):
            g, edge, flip = seams_ref[0, e, f], seams_ref[1, e, f], seams_ref[2, e, f]
            base = jnp.where(edge < 2, 2 * faces + 2 * g + edge, 2 * g + 3 - edge)
            slots[e].append(base + 32 * jnp.where(flip == 1, 1, 0))

    reverse = LANES - 1 - lane
    blocks = side // LANES

    def diffuse(step, carry):
        now = lax.rem(step, 2)
        later = 1 - now

        def extract(i, carry):
            at = pl.multiple_of(8 * i, 8)
            out = jnp.zeros((8, LANES), jnp.float32)
            for f in range(faces):
                u = field[now, f, pl.ds(at + 8, 8), :LANES]
                if side > LANES:
                    u = jnp.where(
                        lane < LANES // 2, u, field[now, f, pl.ds(at + 8, 8), side - LANES :]
                    )
                moved = pltpu.roll(u, 1 + 2 * f, 1)
                out = jnp.where((lane >= 2 * f) & (lane < 2 * f + 2), moved, out)
            columns[pl.ds(at, 8), :] = out
            return carry

        lax.fori_loop(0, side // 8, extract, 0, unroll=side == LANES)
        for b in range(blocks):
            cut = slice(b * LANES, (b + 1) * LANES)
            turned = columns[cut, :].T
            table[: 2 * faces, cut] = turned[: 2 * faces]
        for f in range(faces):
            table[2 * faces + 2 * f : 2 * faces + 2 * f + 1, :] = field[now, f, 8:9, :]
            table[2 * faces + 2 * f + 1 : 2 * faces + 2 * f + 2, :] = field[
                now, f, side + 7 : side + 8, :
            ]
        for b in range(blocks):
            back = blocks - 1 - b
            for r in range(0, 4 * faces, 8):
                value = table[r : r + 8, b * LANES : (b + 1) * LANES]
                table[32 + r : 40 + r, back * LANES : (back + 1) * LANES] = jnp.take_along_axis(
                    value, reverse, axis=1, mode="promise_in_bounds"
                )
        for f in range(faces):
            field[now, f, 7:8, :] = table[pl.ds(slots[0][f], 1), :]
            field[now, f, side + 8 : side + 9, :] = table[pl.ds(slots[1][f], 1), :]
            left, right = 2 * f, (2 * f + LANES - 1) % LANES
            ghosts[left : left + 1, :] = table[pl.ds(slots[2][f], 1), :]
            ghosts[right : right + 1, :] = table[pl.ds(slots[3][f], 1), :]
        for b in range(blocks):
            cut = slice(b * LANES, (b + 1) * LANES)
            ghost_columns[cut, :] = ghosts[:, cut].T

        lanes = lax.broadcasted_iota(jnp.int32, (8, side), 1)
        line_of = lax.broadcasted_iota(jnp.int32, (8, side), 0)

        def update(i, carry):
            at = pl.multiple_of(8 * i, 8)
            line = ghost_columns[pl.ds(at, 8), :]
            for f in range(faces):
                u = field[now, f, pl.ds(at + 8, 8), :]
                if blocks == 1:
                    up = field[now, f, pl.ds(at + 7, 8), :]
                    down = field[now, f, pl.ds(at + 9, 8), :]
                else:
                    before = field[now, f, pl.ds(at, 8), :]
                    after = field[now, f, pl.ds(at + 16, 8), :]
                    up = jnp.where(line_of == 0, pltpu.roll(before, 1, 0), pltpu.roll(u, 1, 0))
                    down = jnp.where(line_of == 7, pltpu.roll(after, 7, 0), pltpu.roll(u, 7, 0))
                ghost = pltpu.roll(line, (LANES - 2 * f) % LANES, 1)
                if blocks > 1:
                    ghost = jnp.concatenate([ghost] * blocks, axis=1)
                left = jnp.where(lanes == 0, ghost, pltpu.roll(u, 1, 1))
                right = jnp.where(lanes == side - 1, ghost, pltpu.roll(u, side - 1, 1))
                total = (up + down) + (left + right)
                field[later, f, pl.ds(at + 8, 8), :] = u + KAPPA * (total - 4.0 * u)
            return carry

        lax.fori_loop(0, side // 8, update, 0, unroll=side == LANES)
        return carry

    lax.fori_loop(0, STEPS, diffuse, 0)

    def divide(i, carry):
        at = pl.multiple_of(8 * i, 8)
        for f in range(faces):
            field[0, f, pl.ds(at + 8, 8), :] = (
                dens[f, pl.ds(at, 8), :] / field[0, f, pl.ds(at + 8, 8), :]
            )
        return carry

    lax.fori_loop(0, side // 8, divide, 0, unroll=side == LANES)
    dual_ref[0] = field[0, :, pl.ds(start + 8, rows), :]
    lax.fori_loop(0, STEPS, diffuse, 0)

    weight = weight_ref[0]
    marginal = scaling_ref[0] * field[0, :, pl.ds(start + 8, rows), :]
    logs[:faces] = weight * jnp.log(marginal)
    logs[faces] = jnp.full((rows, side), weight, jnp.float32)

    def send_logs(i, peer, slot):
        return pltpu.make_async_remote_copy(
            src_ref=logs, dst_ref=others.at[slot],
            send_sem=log_send.at[i], recv_sem=log_recv.at[slot],
            device_id={"member": peer}, device_id_type=MESH,
        )

    partners = [lax.rem(m + i, members) for i in range(1, members)]
    for i, peer in enumerate(partners):
        send_logs(i, peer, m).start()
    total = logs[...]
    for i, peer in enumerate(partners):
        send_logs(i, peer, peer).wait_recv()
        total = total + others[peer]
    bary = jnp.exp(total[:faces] / total[faces:])
    bary_ref[...] = bary
    new_ref[0] = (scaling_ref[0] * bary) / marginal

    for i, peer in enumerate(partners):
        send_logs(i, peer, m).wait_send()
    for peer in peers:
        send_pack(peer, t).wait_send()

    @pl.when(t == 0)
    def _():
        for copy in to_first:
            copy.wait_send()

    @pl.when(t == n - 1)
    def _():
        for copy in to_last:
            copy.wait_send()

    @pl.when(t > 0)
    def _():
        to_above.wait_send()

    @pl.when(t < n - 1)
    def _():
        to_below.wait_send()


def body(density, scaling, member_weights, seams):
    n = lax.axis_size("tile")
    members = lax.axis_size("member")
    _, faces, rows, side = scaling.shape
    groups = faces * rows // 8
    packed = pl.cdiv(groups, LANES // 16) + pl.cdiv(groups, LANES // 8)
    lines = faces + pl.cdiv(faces, 2)
    vmem = functools.partial(pltpu.VMEM, dtype=jnp.float32)
    dma = lambda count: pltpu.SemaphoreType.DMA((count,))
    smem = pl.BlockSpec(memory_space=pltpu.SMEM)
    whole = pl.BlockSpec(memory_space=pltpu.VMEM)
    return pl.pallas_call(
        functools.partial(kernel, n, members, faces, rows, side),
        out_shape=(
            jax.ShapeDtypeStruct(scaling.shape, jnp.float32),
            jax.ShapeDtypeStruct(scaling.shape, jnp.float32),
            jax.ShapeDtypeStruct(scaling.shape[1:], jnp.float32),
        ),
        in_specs=[smem, smem, whole, whole],
        out_specs=(whole, whole, whole),
        scratch_shapes=[
            vmem((2, faces, side + 16, side)),
            vmem((faces, side, side)),
            vmem((packed, 8, LANES)),
            vmem((n, packed, 8, LANES)),
            vmem((lines, 8, side)),
            vmem((lines, 8, side)),
            vmem((lines, 8, side)),
            vmem((lines, 8, side)),
            vmem((lines, 8, side)),
            vmem((lines, 8, side)),
            vmem((64, side)),
            vmem((side, LANES)),
            vmem((LANES, side)),
            vmem((side, LANES)),
            vmem((faces + 1, rows, side)),
            vmem((members, faces + 1, rows, side)),
            dma(n), dma(n), dma(n + 1), dma(n + 1), dma(4), dma(members), dma(members),
        ],
        compiler_params=pltpu.CompilerParams(
            collective_id=0, has_side_effects=True, vmem_limit_bytes=48 << 20
        ),
    )(seams, member_weights, density, scaling)


def solution(mesh):
    return jax.shard_map(
        body,
        mesh=mesh,
        in_specs=(
            P("member", None, "tile", None),
            P("member", None, "tile", None),
            P("member"),
            P(),
        ),
        out_specs=(
            P("member", None, "tile", None),
            P("member", None, "tile", None),
            P(None, "tile", None),
        ),
        check_vma=False,
    )
```

time: 293 us -> 29.4 us (0.10)
  blocking collectives: 240 us -> 0 us
  Pallas kernels: 0 us -> 23.7 us
  starting transfers between devices: 21.7 us -> 0 us
  local copies, waits for them, and re-layouts: 12.9 us -> 4.14 us
  matrix products: 6.02 us -> 0 us
  waiting for transfers between devices: 5.9 us -> 0 us
  other arithmetic: 4.2 us -> 0 us
    psum x9 -> x0, blocking collectives: 240 us -> none  [the longest x8 221 us: edge_table(): return lax.psum(local, 'tile')]
    pallas_call x0 -> x1, Pallas kernels: none -> 23.7 us  [body(): pl.pallas_call(functools.partial(kernel, n, members, faces, rows, side),...]
    ppermute x16 -> x0, starting transfers between devices: 21.7 us -> none  [the longest x8 11.4 us: with_halo(): lax.ppermute(lax.slice_in_dim(block, block.shape[dim] - width, None, axis...]
    dot_general x32 -> x0, matrix products: 6.02 us -> none  [ghost(): jnp.einsum('fq,mqn->mfn', selectors[edge_id], flat, precision=lax.Precisi...]
    ppermute x16 -> x0, waiting for transfers between devices: 5.9 us -> none  [the longest x8 5.88 us: with_halo(): lax.ppermute(lax.slice_in_dim(block, 0, width, axis=dim), axis, backward)]
    slice x30 -> x0, local copies, waits for them, and re-layouts: 2.97 us -> none  [the longest x22 2.34 us: edge_table(): column_pieces = jnp.stack([field[:, :, :, 0], field[:, :, :, -1]], axis=2)]
  transfers between devices with their start and end apart: 16 -> 0, of which waited for: 7 -> 0; matrix products, arithmetic and copies ran while one was open for 3% -> 0% of each run, Pallas kernels for 0% -> 0%
where the time goes in v1:
time: 29.4 us; the launch traced here: 29.1 us
  Pallas kernels  23.7 us (81%)
  local copies, waits for them, and re-layouts  4.14 us (14%)
  between operations  1.3 us (4%)
    pallas_call x1, Pallas kernels, body(): pl.pallas_call(functools.partial(kernel, n, members, faces, rows, side),...  23.7 us
    unnamed x9, local copies, waits for them, and re-layouts  4.14 us

profile of v1, /device:TPU:0, one launch (start us, length us, event | category | flops | bytes accessed | tf_op | source)
XLA Modules:
  0.0 29.1 jit_solution(5292049146954774064)
XLA Ops:
  1.3 0.0 copy-start
  1.3 0.8 %copy-done = f32[1,6,16,128]{3,2,1,0:T(8,128)S(1)} copy-done((f32[1,6,16,128]{3,2,1,0:T(8,128)S(1)}, f32[1,6,16,128]{3,2,1,0:T(8,128)}, u32[]{:S(2)}) %copy-start) | copy-done | bytes 49176
  2.1 0.0 copy-start.1
  2.1 0.8 %copy-done.1 = f32[1,6,16,128]{3,2,1,0:T(8,128)S(1)} copy-done((f32[1,6,16,128]{3,2,1,0:T(8,128)S(1)}, f32[1,6,16,128]{3,2,1,0:T(8,128)}, u32[]{:S(2)}) %copy-start.1) | copy-done | bytes 49176
  2.9 0.0 copy-start.2
  2.9 0.7 %copy-done.2 = s32[3,4,6]{2,1,0:T(4,128)S(1)} copy-done((s32[3,4,6]{2,1,0:T(4,128)S(1)}, s32[3,4,6]{2,1,0:T(4,128)}, u32[]{:S(2)}) %copy-start.2) | copy-done | bytes 312
  3.6 23.7 %shard_map.67 = (f32[1,6,16,128]{3,2,1,0:T(8,128)S(1)}, f32[1,6,16,128]{3,2,1,0:T(8,128)S(1)}, f32[6,16,128]{2,1,0:T(8,128)S(1)}) custom-call(s32[3,4,6]{2,1,0:T(4,128)S(1)} %copy-done.2, f32[1]{0:T(128)S(6)} %copy.10.weight_ref, f32[1,6,16,128]{3,2,1,0:T(8,128)S(1)} %copy-done, f32[1,6,16,128]{3,2,1,0:T(8,128)S(1)} %copy-done.1), custom_call_target="tpu_custom_call" | custom-call | tf_op jit(solution)/shard_map/pallas_call | solution.py:335
  27.3 0.6 %copy.11 = f32[1,6,16,128]{3,2,1,0:T(8,128)} copy(f32[1,6,16,128]{3,2,1,0:T(8,128)S(1)} %get-tuple-element.6) | data formatting | bytes 98304
  27.9 0.6 %copy.12 = f32[1,6,16,128]{3,2,1,0:T(8,128)} copy(f32[1,6,16,128]{3,2,1,0:T(8,128)S(1)} %get-tuple-element.7) | data formatting | bytes 98304
  28.5 0.6 %copy.13 = f32[6,16,128]{2,1,0:T(8,128)} copy(f32[6,16,128]{2,1,0:T(8,128)S(1)} %get-tuple-element.8) | data formatting | bytes 98304
Async XLA Ops:
  1.3 0.8 %copy-start = (f32[1,6,16,128]{3,2,1,0:T(8,128)S(1)}, f32[1,6,16,128]{3,2,1,0:T(8,128)}, u32[]{:S(2)}) copy-start(f32[1,6,16,128]{3,2,1,0:T(8,128)} %density_ref.1) | copy-start | bytes 147460
  2.1 0.8 %copy-start.1 = (f32[1,6,16,128]{3,2,1,0:T(8,128)S(1)}, f32[1,6,16,128]{3,2,1,0:T(8,128)}, u32[]{:S(2)}) copy-start(f32[1,6,16,128]{3,2,1,0:T(8,128)} %scaling_ref.1) | copy-start | bytes 147460
  2.9 0.7 %copy-start.2 = (s32[3,4,6]{2,1,0:T(4,128)S(1)}, s32[3,4,6]{2,1,0:T(4,128)}, u32[]{:S(2)}) copy-start(s32[3,4,6]{2,1,0:T(4,128)} %seams_ref.1) | copy-start | bytes 868

commit v2 on v0

v2 whole, which is shorter than its diff:
```python
import functools

import jax
import jax.numpy as jnp
from jax import lax
from jax.experimental import pallas as pl
from jax.experimental.pallas import tpu as pltpu
from jax.sharding import PartitionSpec as P

STEPS = 4
KAPPA = 0.24
LANES = 128
DEPTH = 8
MESH = pl.DeviceIdType.MESH


def kernel(
    n, members, faces, rows, side,
    seams_ref, weight_ref, density_hbm, scaling_hbm,
    new_ref, dual_ref, bary_ref,
    density, scaling, strips, tile, table, ghosts, ghost_columns,
    pack, packs, first, last, above, below,
    pack_d, packs_d, top_d, bottom_d, first_d, last_d, above_d, below_d,
    logs, others, mine, weights,
    local, pack_send, pack_recv, pack_send_d, pack_recv_d,
    top_send, bottom_send, row_recv, top_send_d, bottom_send_d, row_recv_d,
    log_send, log_recv, weight_send, weight_recv,
):
    t = lax.axis_index("tile")
    m = lax.axis_index("member")
    blocks = side // LANES
    per_block = LANES // rows
    pairs = faces // 2

    barrier = pltpu.get_barrier_semaphore()
    for i in range(1, n):
        pl.semaphore_signal(barrier, inc=1, device_id={"tile": lax.rem(t + i, n)}, device_id_type=MESH)
    for i in range(1, members):
        pl.semaphore_signal(
            barrier, inc=1, device_id={"member": lax.rem(m + i, members)}, device_id_type=MESH
        )
    load_scaling = pltpu.make_async_copy(scaling_hbm.at[0], scaling, local.at[0])
    load_density = pltpu.make_async_copy(density_hbm.at[0], density, local.at[1])
    load_scaling.start()
    load_density.start()

    sub8 = lax.broadcasted_iota(jnp.int32, (8, LANES), 0)
    lane8 = lax.broadcasted_iota(jnp.int32, (8, LANES), 1)
    sub = lax.broadcasted_iota(jnp.int32, (8, side), 0)
    lane = lax.broadcasted_iota(jnp.int32, (8, side), 1)

    def turned_columns(src, at):
        flat = src[:, :, at : at + LANES].reshape(faces * rows, LANES)
        rest = jnp.ones((LANES - faces * rows, LANES), jnp.float32)
        return jnp.concatenate([flat, rest], axis=0).T

    load_scaling.wait()
    turned = turned_columns(scaling, 0)
    pack[0] = turned[:8]
    pack[1] = (turned if blocks == 1 else turned_columns(scaling, side - LANES))[LANES - 8 :]
    packs[t] = pack[...]
    mine[...] = jnp.full((8, LANES), weight_ref[0], jnp.float32)

    peers = [lax.rem(t + i, n) for i in range(1, n)]
    partners = [lax.rem(m + i, members) for i in range(1, members)]

    def remote(src, dst, send, recv, peer, axis="tile"):
        return pltpu.make_async_remote_copy(
            src_ref=src, dst_ref=dst, send_sem=send, recv_sem=recv,
            device_id={axis: peer}, device_id_type=MESH,
        )

    def send_pack(i, slot):
        return remote(pack, packs.at[slot], pack_send.at[i], pack_recv.at[slot], peers[i])

    def send_pack_d(i, slot):
        return remote(pack_d, packs_d.at[slot], pack_send_d.at[i], pack_recv_d.at[slot], peers[i])

    def row_sends(top, bottom, first, last, above, below, top_send, bottom_send, recv):
        up_peer, down_peer = lax.rem(t + n - 1, n), lax.rem(t + 1, n)
        return (
            [remote(top, first, top_send.at[i], recv.at[0], p) for i, p in enumerate(peers)],
            [remote(bottom, last, bottom_send.at[i], recv.at[1], p) for i, p in enumerate(peers)],
            remote(top, below, top_send.at[n], recv.at[2], up_peer),
            remote(bottom, above, bottom_send.at[n], recv.at[3], down_peer),
        )

    lines = row_sends(
        scaling.at[:, pl.ds(0, DEPTH), :], scaling.at[:, pl.ds(rows - DEPTH, DEPTH), :],
        first, last, above, below, top_send, bottom_send, row_recv,
    )
    lines_d = row_sends(
        top_d, bottom_d, first_d, last_d, above_d, below_d, top_send_d, bottom_send_d, row_recv_d
    )

    def on_rows(sends, act):
        to_first, to_last, to_above, to_below = sends

        @pl.when(t == 0)
        def _():
            for copy in reversed(to_first):
                act(copy)

        @pl.when(t == n - 1)
        def _():
            for copy in to_last:
                act(copy)

        @pl.when(t > 0)
        def _():
            act(to_above)

        @pl.when(t < n - 1)
        def _():
            act(to_below)

    def receive_rows(sends):
        to_first, to_last, to_above, to_below = sends

        @pl.when(t > 0)
        def _():
            to_first[0].wait_recv()
            to_below.wait_recv()

        @pl.when(t < n - 1)
        def _():
            to_last[0].wait_recv()
            to_above.wait_recv()

    pl.semaphore_wait(barrier, n - 1 + members - 1)

    on_rows(lines, lambda copy: copy.start())
    for i in range(n - 1):
        send_pack(i, t).start()

    load_density.wait()
    turned = turned_columns(density, 0)
    other = turned if blocks == 1 else turned_columns(density, side - LANES)
    pack_d[...] = jnp.where(sub8 < 4, turned[:8], other[LANES - 8 :])
    packs_d[t] = pack_d[...]
    for j in range(pairs):
        top_d[j] = jnp.where(
            sub < 4, density[2 * j, :8, :], pltpu.roll(density[2 * j + 1, :8, :], 4, 0)
        )
        bottom_d[j] = jnp.where(
            sub >= 4, density[2 * j, rows - 8 :, :], pltpu.roll(density[2 * j + 1, rows - 8 :, :], 4, 0)
        )
    on_rows(lines_d, lambda copy: copy.start())
    for i in range(n - 1):
        send_pack_d(i, t).start()

    def send_weight(i, slot):
        return remote(
            mine, weights.at[slot], weight_send.at[i], weight_recv.at[slot], partners[i], "member"
        )

    for i in range(members - 1):
        send_weight(i, m).start()

    @pl.when(t == 0)
    def _():
        first[...] = scaling[:, :DEPTH, :]
        first_d[...] = top_d[...]
        above[...] = jnp.ones(above.shape, jnp.float32)
        above_d[...] = jnp.ones(above_d.shape, jnp.float32)

    @pl.when(t == n - 1)
    def _():
        last[...] = scaling[:, rows - DEPTH :, :]
        last_d[...] = bottom_d[...]
        below[...] = jnp.ones(below.shape, jnp.float32)
        below_d[...] = jnp.ones(below_d.shape, jnp.float32)

    ghosts[...] = jnp.zeros(ghosts.shape, jnp.float32)
    ghost_columns[...] = jnp.zeros(ghost_columns.shape, jnp.float32)
    table[...] = jnp.zeros(table.shape, jnp.float32)

    slots = []
    for f in range(faces):
        for e in range(4):
            flip = jnp.where(seams_ref[2, e, f] == 1, 32, 0)
            slots.append(4 * seams_ref[0, e, f] + seams_ref[1, e, f] + flip)

    def gather_strip(read, f):
        parts = []
        for b in range(blocks):
            out = jnp.ones((8, LANES), jnp.float32)
            for k in range(per_block):
                shift = (rows * (k - f)) % LANES
                piece = read(b * per_block + k)
                piece = pltpu.roll(piece, shift, 1) if shift else piece
                out = jnp.where((lane8 >= rows * k) & (lane8 < rows * (k + 1)), piece, out)
            parts.append(out)
        return parts[0] if blocks == 1 else jnp.concatenate(parts, axis=1)

    for i in range(n - 1):
        send_pack(i, peers[i]).wait_recv()
    for f in range(faces):
        for k in range(2):
            strips[4 * f + 2 + k] = gather_strip(lambda s: packs[s, k], f)
    receive_rows(lines)
    for f in range(faces):
        strips[4 * f] = first[f]
        strips[4 * f + 1] = last[f]
        tile[f, :8] = above[f]
        tile[f, 8 : 8 + rows] = scaling[f]
        tile[f, 8 + rows :] = below[f]

    start = pl.multiple_of(rows * t, 8)
    reverse = LANES - 1 - lane8
    at_top = (sub == 7) & (t == 0)
    at_bottom = (sub == 0) & (t == n - 1)
    height = (rows + 16) // 8

    def place(line, shift):
        line = pltpu.roll(line, (LANES - shift) % LANES, 1)
        return line if blocks == 1 else jnp.concatenate([line] * blocks, axis=1)

    def stencil(u, up, down, ends):
        left = jnp.where(lane == 0, ends, pltpu.roll(u, 1, 1))
        right = jnp.where(lane == side - 1, ends, pltpu.roll(u, side - 1, 1))
        return u + KAPPA * (((up + down) + (left + right)) - 4.0 * u)

    def diffuse(step, carry):
        for i in range(4 * faces):
            row = 0 if i % 2 == 0 else 7
            table[i : i + 1, :] = strips[i, row : row + 1, :]
        for b in range(blocks):
            back = blocks - 1 - b
            for r in range(0, 4 * faces, 8):
                table[32 + r : 40 + r, back * LANES : (back + 1) * LANES] = jnp.take_along_axis(
                    table[r : r + 8, b * LANES : (b + 1) * LANES], reverse, axis=1,
                    mode="promise_in_bounds",
                )
        for f in range(faces):
            for e in range(4):
                row = 4 * f + 3 - e
                ghosts[row : row + 1, :] = table[pl.ds(slots[4 * f + e], 1), :]
        for b in range(blocks):
            cut = slice(b * LANES, (b + 1) * LANES)
            ghost_columns[8 + b * LANES : 8 + (b + 1) * LANES, :] = ghosts[:, cut].T
        low = ghost_columns[8:16, :]
        high = ghost_columns[side : side + 8, :]

        for f in range(faces):
            for e in range(4):
                u = strips[4 * f + e]
                row = 4 * f + 3 - e
                ghost = jnp.broadcast_to(ghosts[row : row + 1, :], (8, side))
                up, down = pltpu.roll(u, 1, 0), pltpu.roll(u, 7, 0)
                if e % 2 == 0:
                    up = jnp.where(sub == 0, ghost, up)
                else:
                    down = jnp.where(sub == 7, ghost, down)
                ends = place(high if e % 2 else low, 4 * f + 1 + (e // 2) * 2)
                strips[4 * f + e] = stencil(u, up, down, ends)

        for f in range(faces):
            u = [tile[f, 8 * j : 8 * j + 8, :] for j in range(height)]
            over = jnp.broadcast_to(ghosts[4 * f + 3 : 4 * f + 4, :], (8, side))
            under = jnp.broadcast_to(ghosts[4 * f + 2 : 4 * f + 3, :], (8, side))
            u[0] = jnp.where(at_top, over, u[0])
            u[-1] = jnp.where(at_bottom, under, u[-1])
            ups = [pltpu.roll(v, 1, 0) for v in u]
            downs = [pltpu.roll(v, 7, 0) for v in u]
            for j in range(height):
                up = jnp.where(sub == 0, ups[j - 1], ups[j]) if j else ups[j]
                down = jnp.where(sub == 7, downs[j + 1], downs[j]) if j < height - 1 else downs[j]
                ends = place(ghost_columns[pl.ds(start + 8 * j, 8), :], 4 * f + 1)
                tile[f, 8 * j : 8 * j + 8, :] = stencil(u[j], up, down, ends)
        return carry

    lax.fori_loop(0, STEPS, diffuse, 0)

    for i in range(n - 1):
        send_pack_d(i, peers[i]).wait_recv()
    receive_rows(lines_d)
    for f in range(faces):
        columns = gather_strip(lambda s: packs_d[s], f)
        turn = (lambda v: v) if f % 2 == 0 else (lambda v: pltpu.roll(v, 4, 0))
        strips[4 * f] = turn(first_d[f // 2]) / strips[4 * f]
        strips[4 * f + 1] = turn(last_d[f // 2]) / strips[4 * f + 1]
        strips[4 * f + 2] = columns / strips[4 * f + 2]
        strips[4 * f + 3] = columns / strips[4 * f + 3]
        tile[f, :8] = turn(above_d[f // 2]) / tile[f, :8]
        dual = density[f] / tile[f, 8 : 8 + rows]
        tile[f, 8 : 8 + rows] = dual
        dual_ref[0, f] = dual
        tile[f, 8 + rows :] = turn(below_d[f // 2]) / tile[f, 8 + rows :]

    lax.fori_loop(0, STEPS, diffuse, 0)

    marginal = scaling[...] * tile[:, 8 : 8 + rows, :]
    logs[...] = weight_ref[0] * jnp.log(marginal)

    def send_logs(i, slot):
        return remote(logs, others.at[slot], log_send.at[i], log_recv.at[slot], partners[i], "member")

    for i in range(members - 1):
        send_logs(i, m).start()
    weight = mine[...]
    for i in range(members - 1):
        send_weight(i, partners[i]).wait_recv()
        weight = weight + weights[partners[i]]
    if blocks > 1:
        weight = jnp.concatenate([weight] * blocks, axis=1)
    total = logs[...]
    for i in range(members - 1):
        send_logs(i, partners[i]).wait_recv()
        total = total + others[partners[i]]
    bary = jnp.exp(total / weight[:1].reshape(1, 1, side))
    bary_ref[...] = bary
    new_ref[0] = (scaling[...] * bary) / marginal

    for i in range(members - 1):
        send_logs(i, m).wait_send()
        send_weight(i, m).wait_send()
    for i in range(n - 1):
        send_pack(i, t).wait_send()
        send_pack_d(i, t).wait_send()
    on_rows(lines, lambda copy: copy.wait_send())
    on_rows(lines_d, lambda copy: copy.wait_send())


def body(density, scaling, member_weights, seams):
    n = lax.axis_size("tile")
    members = lax.axis_size("member")
    _, faces, rows, side = scaling.shape
    vmem = lambda *shape: pltpu.VMEM(shape, jnp.float32)
    dma = lambda count: pltpu.SemaphoreType.DMA((count,))
    smem = pl.BlockSpec(memory_space=pltpu.SMEM)
    whole = pl.BlockSpec(memory_space=pltpu.VMEM)
    hbm = pl.BlockSpec(memory_space=pltpu.HBM)
    return pl.pallas_call(
        functools.partial(kernel, n, members, faces, rows, side),
        out_shape=(
            jax.ShapeDtypeStruct(scaling.shape, jnp.float32),
            jax.ShapeDtypeStruct(scaling.shape, jnp.float32),
            jax.ShapeDtypeStruct(scaling.shape[1:], jnp.float32),
        ),
        in_specs=[smem, smem, hbm, hbm],
        out_specs=(whole, whole, whole),
        scratch_shapes=[
            vmem(faces, rows, side),
            vmem(faces, rows, side),
            vmem(4 * faces, 8, side),
            vmem(faces, rows + 16, side),
            vmem(64, side),
            vmem(LANES, side),
            vmem(side + 16, LANES),
            vmem(2, 8, LANES),
            vmem(n, 2, 8, LANES),
            *[vmem(faces, DEPTH, side)] * 4,
            vmem(8, LANES),
            vmem(n, 8, LANES),
            *[vmem(faces // 2, 8, side)] * 6,
            vmem(faces, rows, side),
            vmem(members, faces, rows, side),
            vmem(8, LANES),
            vmem(members, 8, LANES),
            dma(2), dma(n), dma(n), dma(n), dma(n),
            dma(n + 1), dma(n + 1), dma(4), dma(n + 1), dma(n + 1), dma(4),
            dma(members), dma(members), dma(members), dma(members),
        ],
        compiler_params=pltpu.CompilerParams(
            collective_id=0, has_side_effects=True
        ),
    )(seams, member_weights, density, scaling)


def solution(mesh):
    return jax.shard_map(
        body,
        mesh=mesh,
        in_specs=(
            P("member", None, "tile", None),
            P("member", None, "tile", None),
            P("member"),
            P(),
        ),
        out_specs=(
            P("member", None, "tile", None),
            P("member", None, "tile", None),
            P(None, "tile", None),
        ),
        check_vma=False,
    )
```

time: 293 us -> 24.3 us (0.08)
  blocking collectives: 240 us -> 0 us
  starting transfers between devices: 21.7 us -> 0 us
  Pallas kernels: 0 us -> 19.8 us
  local copies, waits for them, and re-layouts: 12.9 us -> 2.87 us
  matrix products: 6.02 us -> 0 us
  waiting for transfers between devices: 5.9 us -> 0 us
  other arithmetic: 4.2 us -> 0 us
    psum x9 -> x0, blocking collectives: 240 us -> none  [the longest x8 221 us: edge_table(): return lax.psum(local, 'tile')]
    ppermute x16 -> x0, starting transfers between devices: 21.7 us -> none  [the longest x8 11.4 us: with_halo(): lax.ppermute(lax.slice_in_dim(block, block.shape[dim] - width, None, axis...]
    pallas_call x0 -> x1, Pallas kernels: none -> 19.8 us  [body(): pl.pallas_call(functools.partial(kernel, n, members, faces, rows, side),...]
    dot_general x32 -> x0, matrix products: 6.02 us -> none  [ghost(): jnp.einsum('fq,mqn->mfn', selectors[edge_id], flat, precision=lax.Precisi...]
    ppermute x16 -> x0, waiting for transfers between devices: 5.9 us -> none  [the longest x8 5.88 us: with_halo(): lax.ppermute(lax.slice_in_dim(block, 0, width, axis=dim), axis, backward)]
    slice x30 -> x0, local copies, waits for them, and re-layouts: 2.97 us -> none  [the longest x22 2.34 us: edge_table(): column_pieces = jnp.stack([field[:, :, :, 0], field[:, :, :, -1]], axis=2)]
  transfers between devices with their start and end apart: 16 -> 0, of which waited for: 7 -> 0; matrix products, arithmetic and copies ran while one was open for 3% -> 0% of each run, Pallas kernels for 0% -> 0%
where the time goes in v2:
time: 24.3 us; the launch traced here: 23.9 us
  Pallas kernels  19.8 us (81%)
  local copies, waits for them, and re-layouts  2.87 us (12%)
  between operations  1.3 us (5%)
    pallas_call x1, Pallas kernels, body(): pl.pallas_call(functools.partial(kernel, n, members, faces, rows, side),...  19.8 us
    unnamed x7, local copies, waits for them, and re-layouts  2.87 us

profile of v2, /device:TPU:0, one launch (start us, length us, event | category | flops | bytes accessed | tf_op | source)
XLA Modules:
  0.0 23.9 jit_solution(16617510708665851439)
XLA Ops:
  1.3 19.8 %shard_map.67 = (f32[1,6,16,128]{3,2,1,0:T(8,128)}, f32[1,6,16,128]{3,2,1,0:T(8,128)}, f32[6,16,128]{2,1,0:T(8,128)}) custom-call(s32[3,4,6]{2,1,0:T(4,128)} %seams_ref.1, f32[1]{0:T(128)S(6)} %copy.10.weight_ref, f32[1,6,16,128]{3,2,1,0:T(8,128)} %density_hbm.1, f32[1,6,16,128]{3,2,1,0:T(8,128)} %scaling_hbm.1), custom_call_target="tpu_custom_call" | custom-call | tf_op jit(solution)/shard_map/pallas_call | solution.py:334
  21.0 0.0 copy-start.1
  21.0 1.4 %copy.11 = f32[1,6,16,128]{3,2,1,0:T(8,128)} copy(f32[1,6,16,128]{3,2,1,0:T(8,128)} %get-tuple-element.6) | data formatting | bytes 98304
  22.5 0.0 copy-done.1
  22.5 0.0 copy-start
  22.5 0.6 %copy.12 = f32[1,6,16,128]{3,2,1,0:T(8,128)} copy(f32[1,6,16,128]{3,2,1,0:T(8,128)S(1)} %copy-done.1) | data formatting | bytes 98304
  23.1 0.2 copy-done
  23.3 0.6 %copy.13 = f32[6,16,128]{2,1,0:T(8,128)} copy(f32[6,16,128]{2,1,0:T(8,128)S(1)} %copy-done) | data formatting | bytes 98304
Async XLA Ops:
  21.0 1.4 %copy-start.1 = (f32[1,6,16,128]{3,2,1,0:T(8,128)S(1)}, f32[1,6,16,128]{3,2,1,0:T(8,128)}, u32[]{:S(2)}) copy-start(f32[1,6,16,128]{3,2,1,0:T(8,128)} %get-tuple-element.7) | copy-start | bytes 147460
  22.5 0.8 %copy-start = (f32[6,16,128]{2,1,0:T(8,128)S(1)}, f32[6,16,128]{2,1,0:T(8,128)}, u32[]{:S(2)}) copy-start(f32[6,16,128]{2,1,0:T(8,128)} %get-tuple-element.8) | copy-start | bytes 147460

commit v3 on v2

--- a/solution.py
+++ b/solution.py
@@ -17,8 +17,8 @@
 def kernel(
     n, members, faces, rows, side,
     seams_ref, weight_ref, density_hbm, scaling_hbm,
-    new_ref, dual_ref, bary_ref,
-    density, scaling, strips, tile, table, ghosts, ghost_columns,
+    out_hbm,
+    density, scaling, strips, tile, ghosts, ghost_columns, results,
     pack, packs, first, last, above, below,
     pack_d, packs_d, top_d, bottom_d, first_d, last_d, above_d, below_d,
     logs, others, mine, weights,
@@ -173,13 +173,16 @@
 
     ghosts[...] = jnp.zeros(ghosts.shape, jnp.float32)
     ghost_columns[...] = jnp.zeros(ghost_columns.shape, jnp.float32)
-    table[...] = jnp.zeros(table.shape, jnp.float32)
-
-    slots = []
+
+    where_from = {}
+    row_of = lax.broadcasted_iota(jnp.int32, (32, LANES), 0)
+    flipped = jnp.zeros((32, LANES), jnp.int32)
     for f in range(faces):
         for e in range(4):
-            flip = jnp.where(seams_ref[2, e, f] == 1, 32, 0)
-            slots.append(4 * seams_ref[0, e, f] + seams_ref[1, e, f] + flip)
+            edge = seams_ref[1, e, f]
+            where_from[f, e] = (4 * seams_ref[0, e, f] + edge, 7 * lax.rem(edge, 2))
+            flipped = jnp.where(row_of == 4 * f + 3 - e, seams_ref[2, e, f], flipped)
+    turns = flipped == 1
 
     def gather_strip(read, f):
         parts = []
@@ -222,23 +225,25 @@
         return u + KAPPA * (((up + down) + (left + right)) - 4.0 * u)
 
     def diffuse(step, carry):
-        for i in range(4 * faces):
-            row = 0 if i % 2 == 0 else 7
-            table[i : i + 1, :] = strips[i, row : row + 1, :]
-        for b in range(blocks):
-            back = blocks - 1 - b
-            for r in range(0, 4 * faces, 8):
-                table[32 + r : 40 + r, back * LANES : (back + 1) * LANES] = jnp.take_along_axis(
-                    table[r : r + 8, b * LANES : (b + 1) * LANES], reverse, axis=1,
-                    mode="promise_in_bounds",
-                )
         for f in range(faces):
             for e in range(4):
                 row = 4 * f + 3 - e
-                ghosts[row : row + 1, :] = table[pl.ds(slots[4 * f + e], 1), :]
+                strip, line = where_from[f, e]
+                ghosts[row : row + 1, :] = strips[strip, pl.ds(line, 1), :]
+        lines = [ghosts[:, b * LANES : (b + 1) * LANES] for b in range(blocks)]
         for b in range(blocks):
-            cut = slice(b * LANES, (b + 1) * LANES)
-            ghost_columns[8 + b * LANES : 8 + (b + 1) * LANES, :] = ghosts[:, cut].T
+            backward = jnp.concatenate(
+                [
+                    jnp.take_along_axis(
+                        lines[blocks - 1 - b][r : r + 8], reverse, axis=1, mode="promise_in_bounds"
+                    )
+                    for r in range(0, 32, 8)
+                ],
+                axis=0,
+            )
+            line = jnp.where(turns, backward, lines[b])
+            ghosts[:, b * LANES : (b + 1) * LANES] = line
+            ghost_columns[8 + b * LANES : 8 + (b + 1) * LANES, :32] = line.T
         low = ghost_columns[8:16, :]
         high = ghost_columns[side : side + 8, :]
 
@@ -285,9 +290,11 @@
         tile[f, :8] = turn(above_d[f // 2]) / tile[f, :8]
         dual = density[f] / tile[f, 8 : 8 + rows]
         tile[f, 8 : 8 + rows] = dual
-        dual_ref[0, f] = dual
+        results[1, f] = dual
         tile[f, 8 + rows :] = turn(below_d[f // 2]) / tile[f, 8 + rows :]
 
+    store_dual = pltpu.make_async_copy(results.at[1], out_hbm.at[1], local.at[2])
+    store_dual.start()
     lax.fori_loop(0, STEPS, diffuse, 0)
 
     marginal = scaling[...] * tile[:, 8 : 8 + rows, :]
@@ -309,8 +316,12 @@
         send_logs(i, partners[i]).wait_recv()
         total = total + others[partners[i]]
     bary = jnp.exp(total / weight[:1].reshape(1, 1, side))
-    bary_ref[...] = bary
-    new_ref[0] = (scaling[...] * bary) / marginal
+    results[2] = bary
+    store_bary = pltpu.make_async_copy(results.at[2], out_hbm.at[2], local.at[1])
+    store_bary.start()
+    results[0] = (scaling[...] * bary) / marginal
+    store_new = pltpu.make_async_copy(results.at[0], out_hbm.at[0], local.at[0])
+    store_new.start()
 
     for i in range(members - 1):
         send_logs(i, m).wait_send()
@@ -320,6 +331,21 @@
         send_pack_d(i, t).wait_send()
     on_rows(lines, lambda copy: copy.wait_send())
     on_rows(lines_d, lambda copy: copy.wait_send())
+    store_dual.wait()
+    store_bary.wait()
+    store_new.wait()
+
+
+def hand_out(results, new_hbm, dual_hbm, bary_hbm, sems):
+    copies = [
+        pltpu.make_async_copy(results.at[0], new_hbm.at[0], sems.at[0]),
+        pltpu.make_async_copy(results.at[1], dual_hbm.at[0], sems.at[1]),
+        pltpu.make_async_copy(results.at[2], bary_hbm, sems.at[2]),
+    ]
+    for copy in copies:
+        copy.start()
+    for copy in copies:
+        copy.wait()
 
 
 def body(density, scaling, member_weights, seams):
@@ -329,25 +355,20 @@
     vmem = lambda *shape: pltpu.VMEM(shape, jnp.float32)
     dma = lambda count: pltpu.SemaphoreType.DMA((count,))
     smem = pl.BlockSpec(memory_space=pltpu.SMEM)
-    whole = pl.BlockSpec(memory_space=pltpu.VMEM)
     hbm = pl.BlockSpec(memory_space=pltpu.HBM)
-    return pl.pallas_call(
+    results = pl.pallas_call(
         functools.partial(kernel, n, members, faces, rows, side),
-        out_shape=(
-            jax.ShapeDtypeStruct(scaling.shape, jnp.float32),
-            jax.ShapeDtypeStruct(scaling.shape, jnp.float32),
-            jax.ShapeDtypeStruct(scaling.shape[1:], jnp.float32),
-        ),
+        out_shape=jax.ShapeDtypeStruct((3, faces, rows, side), jnp.float32),
         in_specs=[smem, smem, hbm, hbm],
-        out_specs=(whole, whole, whole),
+        out_specs=hbm,
         scratch_shapes=[
             vmem(faces, rows, side),
             vmem(faces, rows, side),
             vmem(4 * faces, 8, side),
             vmem(faces, rows + 16, side),
-            vmem(64, side),
-            vmem(LANES, side),
+            vmem(32, side),
             vmem(side + 16, LANES),
+            vmem(3, faces, rows, side),
             vmem(2, 8, LANES),
             vmem(n, 2, 8, LANES),
             *[vmem(faces, DEPTH, side)] * 4,
@@ -358,7 +379,7 @@
             vmem(members, faces, rows, side),
             vmem(8, LANES),
             vmem(members, 8, LANES),
-            dma(2), dma(n), dma(n), dma(n), dma(n),
+            dma(3), dma(n), dma(n), dma(n), dma(n),
             dma(n + 1), dma(n + 1), dma(4), dma(n + 1), dma(n + 1), dma(4),
             dma(members), dma(members), dma(members), dma(members),
         ],
@@ -366,6 +387,17 @@
             collective_id=0, has_side_effects=True
         ),
     )(seams, member_weights, density, scaling)
+    return pl.pallas_call(
+        hand_out,
+        out_shape=(
+            jax.ShapeDtypeStruct(scaling.shape, jnp.float32),
+            jax.ShapeDtypeStruct(scaling.shape, jnp.float32),
+            jax.ShapeDtypeStruct(scaling.shape[1:], jnp.float32),
+        ),
+        in_specs=[hbm],
+        out_specs=(hbm, hbm, hbm),
+        scratch_shapes=[dma(3)],
+    )(results)
 
 
 def solution(mesh):

time: 24.3 us -> 26.7 us (1.099)
  Pallas kernels: 19.8 us -> 25.2 us
  local copies, waits for them, and re-layouts: 2.87 us -> 0 us
    pallas_call x0 -> x1, Pallas kernels: none -> 5.6 us  [body(): pl.pallas_call(hand_out, out_shape=(jax.ShapeDtypeStruct(scaling.shape, j...]
    unnamed x7 -> x0, local copies, waits for them, and re-layouts: 2.87 us -> none
where the time goes in v3:
time: 26.7 us; the launch traced here: 26.5 us
  Pallas kernels  25.2 us (94%)
  between operations  1.29 us (5%)
    pallas_call x1, Pallas kernels, body(): pl.pallas_call(functools.partial(kernel, n, members, faces, rows, side),...  19.6 us
    pallas_call x1, Pallas kernels, body(): pl.pallas_call(hand_out, out_shape=(jax.ShapeDtypeStruct(scaling.shape, j...  5.6 us

profile of v3, /device:TPU:0, one launch (start us, length us, event | category | flops | bytes accessed | tf_op | source)
XLA Modules:
  0.0 26.5 jit_solution(2476993719421687595)
XLA Ops:
  1.3 19.6 %shard_map.67.results = f32[3,6,16,128]{3,2,1,0:T(8,128)} custom-call(s32[3,4,6]{2,1,0:T(4,128)} %seams_ref.1, f32[1]{0:T(128)S(6)} %copy.7.weight_ref, f32[1,6,16,128]{3,2,1,0:T(8,128)} %density_hbm.1, f32[1,6,16,128]{3,2,1,0:T(8,128)} %scaling_hbm.1), custom_call_target="tpu_custom_call" | custom-call | tf_op jit(solution)/shard_map/pallas_call | solution.py:359
  20.9 5.6 %shard_map.68 = (f32[1,6,16,128]{3,2,1,0:T(8,128)}, f32[1,6,16,128]{3,2,1,0:T(8,128)}, f32[6,16,128]{2,1,0:T(8,128)}) custom-call(f32[3,6,16,128]{3,2,1,0:T(8,128)} %shard_map.67.results), custom_call_target="tpu_custom_call" | custom-call | tf_op jit(solution)/shard_map/pallas_call | solution.py:390

commit v4 on v3

--- a/solution.py
+++ b/solution.py
@@ -32,6 +32,9 @@
     per_block = LANES // rows
     pairs = faces // 2
 
+    packs[...] = jnp.ones(packs.shape, jnp.float32)
+    packs_d[...] = jnp.ones(packs_d.shape, jnp.float32)
+
     barrier = pltpu.get_barrier_semaphore()
     for i in range(1, n):
         pl.semaphore_signal(barrier, inc=1, device_id={"tile": lax.rem(t + i, n)}, device_id_type=MESH)
@@ -75,6 +78,18 @@
 
     def send_pack_d(i, slot):
         return remote(pack_d, packs_d.at[slot], pack_send_d.at[i], pack_recv_d.at[slot], peers[i])
+
+    def reaches(source, target):
+        mirror = n - 1 - target
+        ends = (target == 0) | (target == n - 1)
+        return ends | (jnp.abs(source - target) <= 1) | (jnp.abs(source - mirror) <= 1)
+
+    def on_packs(sends, act, arriving):
+        for i in range(n - 1):
+
+            @pl.when(reaches(peers[i], t) if arriving else reaches(t, peers[i]))
+            def _():
+                act(sends(i, peers[i] if arriving else t))
 
     def row_sends(top, bottom, first, last, above, below, top_send, bottom_send, recv):
         up_peer, down_peer = lax.rem(t + n - 1, n), lax.rem(t + 1, n)
@@ -129,9 +144,8 @@
 
     pl.semaphore_wait(barrier, n - 1 + members - 1)
 
+    on_packs(send_pack, lambda copy: copy.start(), False)
     on_rows(lines, lambda copy: copy.start())
-    for i in range(n - 1):
-        send_pack(i, t).start()
 
     load_density.wait()
     turned = turned_columns(density, 0)
@@ -145,9 +159,8 @@
         bottom_d[j] = jnp.where(
             sub >= 4, density[2 * j, rows - 8 :, :], pltpu.roll(density[2 * j + 1, rows - 8 :, :], 4, 0)
         )
+    on_packs(send_pack_d, lambda copy: copy.start(), False)
     on_rows(lines_d, lambda copy: copy.start())
-    for i in range(n - 1):
-        send_pack_d(i, t).start()
 
     def send_weight(i, slot):
         return remote(
@@ -196,8 +209,7 @@
             parts.append(out)
         return parts[0] if blocks == 1 else jnp.concatenate(parts, axis=1)
 
-    for i in range(n - 1):
-        send_pack(i, peers[i]).wait_recv()
+    on_packs(send_pack, lambda copy: copy.wait_recv(), True)
     for f in range(faces):
         for k in range(2):
             strips[4 * f + 2 + k] = gather_strip(lambda s: packs[s, k], f)
@@ -277,8 +289,7 @@
 
     lax.fori_loop(0, STEPS, diffuse, 0)
 
-    for i in range(n - 1):
-        send_pack_d(i, peers[i]).wait_recv()
+    on_packs(send_pack_d, lambda copy: copy.wait_recv(), True)
     receive_rows(lines_d)
     for f in range(faces):
         columns = gather_strip(lambda s: packs_d[s], f)
@@ -326,9 +337,8 @@
     for i in range(members - 1):
         send_logs(i, m).wait_send()
         send_weight(i, m).wait_send()
-    for i in range(n - 1):
-        send_pack(i, t).wait_send()
-        send_pack_d(i, t).wait_send()
+    on_packs(send_pack, lambda copy: copy.wait_send(), False)
+    on_packs(send_pack_d, lambda copy: copy.wait_send(), False)
     on_rows(lines, lambda copy: copy.wait_send())
     on_rows(lines_d, lambda copy: copy.wait_send())
     store_dual.wait()
@@ -336,16 +346,17 @@
     store_new.wait()
 
 
-def hand_out(results, new_hbm, dual_hbm, bary_hbm, sems):
-    copies = [
-        pltpu.make_async_copy(results.at[0], new_hbm.at[0], sems.at[0]),
-        pltpu.make_async_copy(results.at[1], dual_hbm.at[0], sems.at[1]),
-        pltpu.make_async_copy(results.at[2], bary_hbm, sems.at[2]),
-    ]
-    for copy in copies:
-        copy.start()
-    for copy in copies:
-        copy.wait()
+def hand_out(results, new_hbm, dual_hbm, bary_hbm, held, loaded, stored):
+    targets = (new_hbm.at[0], dual_hbm.at[0], bary_hbm)
+    loads = [pltpu.make_async_copy(results.at[i], held.at[i], loaded.at[i]) for i in range(3)]
+    stores = [pltpu.make_async_copy(held.at[i], targets[i], stored.at[i]) for i in range(3)]
+    for load in loads:
+        load.start()
+    for load, store in zip(loads, stores):
+        load.wait()
+        store.start()
+    for store in stores:
+        store.wait()
 
 
 def body(density, scaling, member_weights, seams):
@@ -396,7 +407,7 @@
         ),
         in_specs=[hbm],
         out_specs=(hbm, hbm, hbm),
-        scratch_shapes=[dma(3)],
+        scratch_shapes=[vmem(3, faces, rows, side), dma(3), dma(3)],
     )(results)
 
 

time: 26.7 us -> 21.8 us (0.82)
  Pallas kernels: 25.2 us -> 20.2 us
    pallas_call x1, Pallas kernels: 5.6 us -> 1.52 us  [body(): pl.pallas_call(hand_out, out_shape=(jax.ShapeDtypeStruct(scaling.shape, j...]
    pallas_call x1, Pallas kernels: 19.6 us -> 18.7 us  [body(): pl.pallas_call(functools.partial(kernel, n, members, faces, rows, side),...]
where the time goes in v4:
time: 21.8 us; the launch traced here: 21.5 us
  Pallas kernels  20.2 us (93%)
  between operations  1.29 us (6%)
    pallas_call x1, Pallas kernels, body(): pl.pallas_call(functools.partial(kernel, n, members, faces, rows, side),...  18.7 us
    pallas_call x1, Pallas kernels, body(): pl.pallas_call(hand_out, out_shape=(jax.ShapeDtypeStruct(scaling.shape, j...  1.52 us

profile of v4, /device:TPU:0, one launch (start us, length us, event | category | flops | bytes accessed | tf_op | source)
XLA Modules:
  0.0 21.5 jit_solution(11299911590893923015)
XLA Ops:
  1.3 18.7 %shard_map.67.results = f32[3,6,16,128]{3,2,1,0:T(8,128)} custom-call(s32[3,4,6]{2,1,0:T(4,128)} %seams_ref.1, f32[1]{0:T(128)S(6)} %copy.7.weight_ref, f32[1,6,16,128]{3,2,1,0:T(8,128)} %density_hbm.1, f32[1,6,16,128]{3,2,1,0:T(8,128)} %scaling_hbm.1), custom_call_target="tpu_custom_call" | custom-call | tf_op jit(solution)/shard_map/pallas_call | solution.py:370
  20.0 1.5 %shard_map.68 = (f32[1,6,16,128]{3,2,1,0:T(8,128)}, f32[1,6,16,128]{3,2,1,0:T(8,128)}, f32[6,16,128]{2,1,0:T(8,128)}) custom-call(f32[3,6,16,128]{3,2,1,0:T(8,128)} %shard_map.67.results), custom_call_target="tpu_custom_call" | custom-call | tf_op jit(solution)/shard_map/pallas_call | solution.py:401

commit v5 on v4

--- a/solution.py
+++ b/solution.py
@@ -187,13 +187,15 @@
     ghosts[...] = jnp.zeros(ghosts.shape, jnp.float32)
     ghost_columns[...] = jnp.zeros(ghost_columns.shape, jnp.float32)
 
-    where_from = {}
-    row_of = lax.broadcasted_iota(jnp.int32, (32, LANES), 0)
-    flipped = jnp.zeros((32, LANES), jnp.int32)
+    whole_line, merged_line = {}, {}
+    row_of = lax.broadcasted_iota(jnp.int32, (24, LANES), 0)
+    flipped = jnp.zeros((24, LANES), jnp.int32)
     for f in range(faces):
         for e in range(4):
-            edge = seams_ref[1, e, f]
-            where_from[f, e] = (4 * seams_ref[0, e, f] + edge, 7 * lax.rem(edge, 2))
+            face, edge = seams_ref[0, e, f], seams_ref[1, e, f]
+            second = lax.rem(edge, 2)
+            whole_line[f, e] = 32 * face + 8 * edge + 7 * second
+            merged_line[f, e] = 16 * face + 4 * (edge - second) + 7 * second
             flipped = jnp.where(row_of == 4 * f + 3 - e, seams_ref[2, e, f], flipped)
     turns = flipped == 1
 
@@ -212,11 +214,12 @@
     on_packs(send_pack, lambda copy: copy.wait_recv(), True)
     for f in range(faces):
         for k in range(2):
-            strips[4 * f + 2 + k] = gather_strip(lambda s: packs[s, k], f)
+            at = 32 * f + 16 + 8 * k
+            strips[at : at + 8, :] = gather_strip(lambda s: packs[s, k], f)
     receive_rows(lines)
     for f in range(faces):
-        strips[4 * f] = first[f]
-        strips[4 * f + 1] = last[f]
+        strips[32 * f : 32 * f + 8, :] = first[f]
+        strips[32 * f + 8 : 32 * f + 16, :] = last[f]
         tile[f, :8] = above[f]
         tile[f, 8 : 8 + rows] = scaling[f]
         tile[f, 8 + rows :] = below[f]
@@ -236,77 +239,114 @@
         right = jnp.where(lane == side - 1, ends, pltpu.roll(u, side - 1, 1))
         return u + KAPPA * (((up + down) + (left + right)) - 4.0 * u)
 
-    def diffuse(step, carry):
+    def read_ghosts(line_of):
         for f in range(faces):
             for e in range(4):
                 row = 4 * f + 3 - e
-                strip, line = where_from[f, e]
-                ghosts[row : row + 1, :] = strips[strip, pl.ds(line, 1), :]
-        lines = [ghosts[:, b * LANES : (b + 1) * LANES] for b in range(blocks)]
+                ghosts[row : row + 1, :] = strips[pl.ds(line_of[f, e], 1), :]
+        lines = [ghosts[: 4 * faces, b * LANES : (b + 1) * LANES] for b in range(blocks)]
+        rest = jnp.zeros((32 - 4 * faces, LANES), jnp.float32)
         for b in range(blocks):
             backward = jnp.concatenate(
                 [
                     jnp.take_along_axis(
                         lines[blocks - 1 - b][r : r + 8], reverse, axis=1, mode="promise_in_bounds"
                     )
-                    for r in range(0, 32, 8)
+                    for r in range(0, 4 * faces, 8)
                 ],
                 axis=0,
             )
             line = jnp.where(turns, backward, lines[b])
-            ghosts[:, b * LANES : (b + 1) * LANES] = line
-            ghost_columns[8 + b * LANES : 8 + (b + 1) * LANES, :32] = line.T
-        low = ghost_columns[8:16, :]
-        high = ghost_columns[side : side + 8, :]
-
+            ghosts[: 4 * faces, b * LANES : (b + 1) * LANES] = line
+            at = 8 + b * LANES
+            ghost_columns[at : at + LANES, :32] = jnp.concatenate([line, rest], axis=0).T
+
+    def ghost_row(f, e):
+        row = 4 * f + 3 - e
+        return jnp.broadcast_to(ghosts[row : row + 1, :], (8, side))
+
+    def advance(u, first_rows, last_rows, over, under, columns, shift):
+        up, down = first_rows, last_rows
+        if over is not None:
+            up = jnp.where(sub == 0, over, up)
+        if under is not None:
+            down = jnp.where(sub == 7, under, down)
+        return stencil(u, up, down, place(columns, shift))
+
+    def advance_tile(f, u, columns, closed):
+        count = len(u)
+        ups = [pltpu.roll(v, 1, 0) for v in u]
+        downs = [pltpu.roll(v, 7, 0) for v in u]
+        result = []
+        for j in range(count):
+            before = ups[j - 1] if j or closed else None
+            after = downs[(j + 1) % count] if j < count - 1 or closed else None
+            result.append(advance(u[j], ups[j], downs[j], before, after, columns[j], 4 * f + 1))
+        return result
+
+    def diffuse(step, carry):
+        read_ghosts(whole_line)
+        ends = (ghost_columns[8:16, :], ghost_columns[side : side + 8, :])
         for f in range(faces):
             for e in range(4):
-                u = strips[4 * f + e]
-                row = 4 * f + 3 - e
-                ghost = jnp.broadcast_to(ghosts[row : row + 1, :], (8, side))
-                up, down = pltpu.roll(u, 1, 0), pltpu.roll(u, 7, 0)
-                if e % 2 == 0:
-                    up = jnp.where(sub == 0, ghost, up)
-                else:
-                    down = jnp.where(sub == 7, ghost, down)
-                ends = place(high if e % 2 else low, 4 * f + 1 + (e // 2) * 2)
-                strips[4 * f + e] = stencil(u, up, down, ends)
-
+                at = 32 * f + 8 * e
+                u = strips[at : at + 8, :]
+                ghost = ghost_row(f, e)
+                over, under = (None, ghost) if e % 2 else (ghost, None)
+                strips[at : at + 8, :] = advance(
+                    u, pltpu.roll(u, 1, 0), pltpu.roll(u, 7, 0), over, under,
+                    ends[e % 2], 4 * f + 1 + (e // 2) * 2,
+                )
         for f in range(faces):
             u = [tile[f, 8 * j : 8 * j + 8, :] for j in range(height)]
-            over = jnp.broadcast_to(ghosts[4 * f + 3 : 4 * f + 4, :], (8, side))
-            under = jnp.broadcast_to(ghosts[4 * f + 2 : 4 * f + 3, :], (8, side))
-            u[0] = jnp.where(at_top, over, u[0])
-            u[-1] = jnp.where(at_bottom, under, u[-1])
-            ups = [pltpu.roll(v, 1, 0) for v in u]
-            downs = [pltpu.roll(v, 7, 0) for v in u]
-            for j in range(height):
-                up = jnp.where(sub == 0, ups[j - 1], ups[j]) if j else ups[j]
-                down = jnp.where(sub == 7, downs[j + 1], downs[j]) if j < height - 1 else downs[j]
-                ends = place(ghost_columns[pl.ds(start + 8 * j, 8), :], 4 * f + 1)
-                tile[f, 8 * j : 8 * j + 8, :] = stencil(u[j], up, down, ends)
+            u[0] = jnp.where(at_top, ghost_row(f, 0), u[0])
+            u[-1] = jnp.where(at_bottom, ghost_row(f, 1), u[-1])
+            columns = [ghost_columns[pl.ds(start + 8 * j, 8), :] for j in range(height)]
+            for j, value in enumerate(advance_tile(f, u, columns, False)):
+                tile[f, 8 * j : 8 * j + 8, :] = value
+        return carry
+
+    def diffuse_merged(step, carry):
+        read_ghosts(merged_line)
+        ends = jnp.where(sub8 < 4, ghost_columns[8:16, :], ghost_columns[side : side + 8, :])
+        for f in range(faces):
+            for k in range(2):
+                at = 16 * f + 8 * k
+                u = strips[at : at + 8, :]
+                strips[at : at + 8, :] = advance(
+                    u, pltpu.roll(u, 1, 0), pltpu.roll(u, 7, 0),
+                    ghost_row(f, 2 * k), ghost_row(f, 2 * k + 1), ends, 4 * f + 1 + 2 * k,
+                )
+        columns = [ghost_columns[pl.ds(start + 8 * j, 8), :] for j in range(height)]
+        columns = columns[1:-1] + [jnp.where(sub8 < 4, columns[-1], columns[0])]
+        for f in range(faces):
+            u = [tile[f, 8 * j : 8 * j + 8, :] for j in range(1, height)]
+            u[-1] = jnp.where(at_top, ghost_row(f, 0), u[-1])
+            u[-1] = jnp.where(at_bottom, ghost_row(f, 1), u[-1])
+            for j, value in enumerate(advance_tile(f, u, columns, True)):
+                tile[f, 8 * j + 8 : 8 * j + 16, :] = value
         return carry
 
     lax.fori_loop(0, STEPS, diffuse, 0)
 
     on_packs(send_pack_d, lambda copy: copy.wait_recv(), True)
     receive_rows(lines_d)
+    upper = sub < 4
     for f in range(faces):
-        columns = gather_strip(lambda s: packs_d[s], f)
         turn = (lambda v: v) if f % 2 == 0 else (lambda v: pltpu.roll(v, 4, 0))
-        strips[4 * f] = turn(first_d[f // 2]) / strips[4 * f]
-        strips[4 * f + 1] = turn(last_d[f // 2]) / strips[4 * f + 1]
-        strips[4 * f + 2] = columns / strips[4 * f + 2]
-        strips[4 * f + 3] = columns / strips[4 * f + 3]
-        tile[f, :8] = turn(above_d[f // 2]) / tile[f, :8]
-        dual = density[f] / tile[f, 8 : 8 + rows]
-        tile[f, 8 : 8 + rows] = dual
+        whole = [strips[32 * f + 8 * e : 32 * f + 8 * e + 8, :] for e in range(4)]
+        edge_rows = jnp.where(upper, turn(first_d[f // 2]), turn(last_d[f // 2]))
+        edge_columns = gather_strip(lambda s: packs_d[s], f)
+        strips[16 * f : 16 * f + 8, :] = edge_rows / jnp.where(upper, whole[0], whole[1])
+        strips[16 * f + 8 : 16 * f + 16, :] = edge_columns / jnp.where(upper, whole[2], whole[3])
+        around = jnp.where(upper, turn(below_d[f // 2]), turn(above_d[f // 2]))
+        dual = density[f] / tile[f, 8 : 8 + rows, :]
+        tile[f, 8 + rows :, :] = around / jnp.where(upper, tile[f, 8 + rows :, :], tile[f, :8, :])
+        tile[f, 8 : 8 + rows, :] = dual
         results[1, f] = dual
-        tile[f, 8 + rows :] = turn(below_d[f // 2]) / tile[f, 8 + rows :]
-
     store_dual = pltpu.make_async_copy(results.at[1], out_hbm.at[1], local.at[2])
     store_dual.start()
-    lax.fori_loop(0, STEPS, diffuse, 0)
+    lax.fori_loop(0, STEPS, diffuse_merged, 0)
 
     marginal = scaling[...] * tile[:, 8 : 8 + rows, :]
     logs[...] = weight_ref[0] * jnp.log(marginal)
@@ -375,7 +415,7 @@
         scratch_shapes=[
             vmem(faces, rows, side),
             vmem(faces, rows, side),
-            vmem(4 * faces, 8, side),
+            vmem(32 * faces, side),
             vmem(faces, rows + 16, side),
             vmem(32, side),
             vmem(side + 16, LANES),

time: 21.8 us -> 21.6 us (level)
  no operation moved by 1% of the time
where the time goes in v5:
time: 21.6 us; the launch traced here: 21.3 us
  Pallas kernels  20 us (93%)
  between operations  1.29 us (6%)
    pallas_call x1, Pallas kernels, body(): pl.pallas_call(functools.partial(kernel, n, members, faces, rows, side),...  18.5 us
    pallas_call x1, Pallas kernels, body(): pl.pallas_call(hand_out, out_shape=(jax.ShapeDtypeStruct(scaling.shape, j...  1.52 us

profile of v5, /device:TPU:0, one launch (start us, length us, event | category | flops | bytes accessed | tf_op | source)
XLA Modules:
  0.0 21.3 jit_solution(43966006001429612)
XLA Ops:
  1.3 18.5 %shard_map.67.results = f32[3,6,16,128]{3,2,1,0:T(8,128)} custom-call(s32[3,4,6]{2,1,0:T(4,128)} %seams_ref.1, f32[1]{0:T(128)S(6)} %copy.7.weight_ref, f32[1,6,16,128]{3,2,1,0:T(8,128)} %density_hbm.1, f32[1,6,16,128]{3,2,1,0:T(8,128)} %scaling_hbm.1), custom_call_target="tpu_custom_call" | custom-call | tf_op jit(solution)/shard_map/pallas_call | solution.py:410
  19.8 1.5 %shard_map.68 = (f32[1,6,16,128]{3,2,1,0:T(8,128)}, f32[1,6,16,128]{3,2,1,0:T(8,128)}, f32[6,16,128]{2,1,0:T(8,128)}) custom-call(f32[3,6,16,128]{3,2,1,0:T(8,128)} %shard_map.67.results), custom_call_target="tpu_custom_call" | custom-call | tf_op jit(solution)/shard_map/pallas_call | solution.py:441

commit v6 on v5

--- a/solution.py
+++ b/solution.py
@@ -16,9 +16,9 @@
 
 def kernel(
     n, members, faces, rows, side,
-    seams_ref, weight_ref, density_hbm, scaling_hbm,
+    seams_hbm, weight_hbm, density_hbm, scaling_hbm,
     out_hbm,
-    density, scaling, strips, tile, ghosts, ghost_columns, results,
+    seams_ref, weight_ref, density, scaling, strips, tile, ghosts, ghost_columns, results,
     pack, packs, first, last, above, below,
     pack_d, packs_d, top_d, bottom_d, first_d, last_d, above_d, below_d,
     logs, others, mine, weights,
@@ -46,6 +46,10 @@
     load_density = pltpu.make_async_copy(density_hbm.at[0], density, local.at[1])
     load_scaling.start()
     load_density.start()
+    load_weight = pltpu.make_async_copy(weight_hbm, weight_ref, local.at[3])
+    load_seams = pltpu.make_async_copy(seams_hbm, seams_ref, local.at[4])
+    load_weight.start()
+    load_seams.start()
 
     sub8 = lax.broadcasted_iota(jnp.int32, (8, LANES), 0)
     lane8 = lax.broadcasted_iota(jnp.int32, (8, LANES), 1)
@@ -57,12 +61,6 @@
         rest = jnp.ones((LANES - faces * rows, LANES), jnp.float32)
         return jnp.concatenate([flat, rest], axis=0).T
 
-    load_scaling.wait()
-    turned = turned_columns(scaling, 0)
-    pack[0] = turned[:8]
-    pack[1] = (turned if blocks == 1 else turned_columns(scaling, side - LANES))[LANES - 8 :]
-    packs[t] = pack[...]
-    mine[...] = jnp.full((8, LANES), weight_ref[0], jnp.float32)
 
     peers = [lax.rem(t + i, n) for i in range(1, n)]
     partners = [lax.rem(m + i, members) for i in range(1, members)]
@@ -142,11 +140,11 @@
             to_last[0].wait_recv()
             to_above.wait_recv()
 
-    pl.semaphore_wait(barrier, n - 1 + members - 1)
-
-    on_packs(send_pack, lambda copy: copy.start(), False)
-    on_rows(lines, lambda copy: copy.start())
-
+    load_scaling.wait()
+    turned = turned_columns(scaling, 0)
+    pack[0] = turned[:8]
+    pack[1] = (turned if blocks == 1 else turned_columns(scaling, side - LANES))[LANES - 8 :]
+    packs[t] = pack[...]
     load_density.wait()
     turned = turned_columns(density, 0)
     other = turned if blocks == 1 else turned_columns(density, side - LANES)
@@ -159,6 +157,11 @@
         bottom_d[j] = jnp.where(
             sub >= 4, density[2 * j, rows - 8 :, :], pltpu.roll(density[2 * j + 1, rows - 8 :, :], 4, 0)
         )
+    pl.semaphore_wait(barrier, n - 1 + members - 1)
+
+    on_packs(send_pack, lambda copy: copy.start(), False)
+    on_rows(lines, lambda copy: copy.start())
+
     on_packs(send_pack_d, lambda copy: copy.start(), False)
     on_rows(lines_d, lambda copy: copy.start())
 
@@ -167,6 +170,8 @@
             mine, weights.at[slot], weight_send.at[i], weight_recv.at[slot], partners[i], "member"
         )
 
+    load_weight.wait()
+    mine[...] = jnp.full((8, LANES), weight_ref[0], jnp.float32)
     for i in range(members - 1):
         send_weight(i, m).start()
 
@@ -187,6 +192,7 @@
     ghosts[...] = jnp.zeros(ghosts.shape, jnp.float32)
     ghost_columns[...] = jnp.zeros(ghost_columns.shape, jnp.float32)
 
+    load_seams.wait()
     whole_line, merged_line = {}, {}
     row_of = lax.broadcasted_iota(jnp.int32, (24, LANES), 0)
     flipped = jnp.zeros((24, LANES), jnp.int32)
@@ -405,14 +411,15 @@
     _, faces, rows, side = scaling.shape
     vmem = lambda *shape: pltpu.VMEM(shape, jnp.float32)
     dma = lambda count: pltpu.SemaphoreType.DMA((count,))
-    smem = pl.BlockSpec(memory_space=pltpu.SMEM)
     hbm = pl.BlockSpec(memory_space=pltpu.HBM)
     results = pl.pallas_call(
         functools.partial(kernel, n, members, faces, rows, side),
         out_shape=jax.ShapeDtypeStruct((3, faces, rows, side), jnp.float32),
-        in_specs=[smem, smem, hbm, hbm],
+        in_specs=[hbm] * 4,
         out_specs=hbm,
         scratch_shapes=[
+            pltpu.SMEM(seams.shape, jnp.int32),
+            pltpu.SMEM(member_weights.shape, jnp.float32),
             vmem(faces, rows, side),
             vmem(faces, rows, side),
             vmem(32 * faces, side),
@@ -430,7 +437,7 @@
             vmem(members, faces, rows, side),
             vmem(8, LANES),
             vmem(members, 8, LANES),
-            dma(3), dma(n), dma(n), dma(n), dma(n),
+            dma(5), dma(n), dma(n), dma(n), dma(n),
             dma(n + 1), dma(n + 1), dma(4), dma(n + 1), dma(n + 1), dma(4),
             dma(members), dma(members), dma(members), dma(members),
         ],

time: 21.6 us -> 20.7 us (0.958)
  Pallas kernels: 20 us -> 19.2 us
    pallas_call x1, Pallas kernels: 18.5 us -> 17.7 us  [body(): pl.pallas_call(functools.partial(kernel, n, members, faces, rows, side),...]
where the time goes in v6:
time: 20.7 us; the launch traced here: 20.5 us
  Pallas kernels  19.2 us (93%)
  between operations  1.29 us (6%)
    pallas_call x1, Pallas kernels, body(): pl.pallas_call(functools.partial(kernel, n, members, faces, rows, side),...  17.7 us
    pallas_call x1, Pallas kernels, body(): pl.pallas_call(hand_out, out_shape=(jax.ShapeDtypeStruct(scaling.shape, j...  1.52 us

profile of v6, /device:TPU:0, one launch (start us, length us, event | category | flops | bytes accessed | tf_op | source)
XLA Modules:
  0.0 20.5 jit_solution(8148864479474733490)
XLA Ops:
  1.3 17.7 %shard_map.67.results = f32[3,6,16,128]{3,2,1,0:T(8,128)} custom-call(s32[3,4,6]{2,1,0:T(4,128)} %seams_hbm.1, f32[1]{0:T(128)S(6)} %copy.7.weight_hbm, f32[1,6,16,128]{3,2,1,0:T(8,128)} %density_hbm.1, f32[1,6,16,128]{3,2,1,0:T(8,128)} %scaling_hbm.1), custom_call_target="tpu_custom_call" | custom-call | tf_op jit(solution)/shard_map/pallas_call | solution.py:415
  19.0 1.5 %shard_map.68 = (f32[1,6,16,128]{3,2,1,0:T(8,128)}, f32[1,6,16,128]{3,2,1,0:T(8,128)}, f32[6,16,128]{2,1,0:T(8,128)}) custom-call(f32[3,6,16,128]{3,2,1,0:T(8,128)} %shard_map.67.results), custom_call_target="tpu_custom_call" | custom-call | tf_op jit(solution)/shard_map/pallas_call | solution.py:448

commit v7 on v6

--- a/solution.py
+++ b/solution.py
@@ -20,9 +20,9 @@
     out_hbm,
     seams_ref, weight_ref, density, scaling, strips, tile, ghosts, ghost_columns, results,
     pack, packs, first, last, above, below,
-    pack_d, packs_d, top_d, bottom_d, first_d, last_d, above_d, below_d,
+    top_d, bottom_d, first_d, last_d, above_d, below_d,
     logs, others, mine, weights,
-    local, pack_send, pack_recv, pack_send_d, pack_recv_d,
+    local, pack_send, pack_recv,
     top_send, bottom_send, row_recv, top_send_d, bottom_send_d, row_recv_d,
     log_send, log_recv, weight_send, weight_recv,
 ):
@@ -33,7 +33,6 @@
     pairs = faces // 2
 
     packs[...] = jnp.ones(packs.shape, jnp.float32)
-    packs_d[...] = jnp.ones(packs_d.shape, jnp.float32)
 
     barrier = pltpu.get_barrier_semaphore()
     for i in range(1, n):
@@ -74,9 +73,6 @@
     def send_pack(i, slot):
         return remote(pack, packs.at[slot], pack_send.at[i], pack_recv.at[slot], peers[i])
 
-    def send_pack_d(i, slot):
-        return remote(pack_d, packs_d.at[slot], pack_send_d.at[i], pack_recv_d.at[slot], peers[i])
-
     def reaches(source, target):
         mirror = n - 1 - target
         ends = (target == 0) | (target == n - 1)
@@ -144,12 +140,11 @@
     turned = turned_columns(scaling, 0)
     pack[0] = turned[:8]
     pack[1] = (turned if blocks == 1 else turned_columns(scaling, side - LANES))[LANES - 8 :]
-    packs[t] = pack[...]
     load_density.wait()
     turned = turned_columns(density, 0)
     other = turned if blocks == 1 else turned_columns(density, side - LANES)
-    pack_d[...] = jnp.where(sub8 < 4, turned[:8], other[LANES - 8 :])
-    packs_d[t] = pack_d[...]
+    pack[2] = jnp.where(sub8 < 4, turned[:8], other[LANES - 8 :])
+    packs[t] = pack[...]
     for j in range(pairs):
         top_d[j] = jnp.where(
             sub < 4, density[2 * j, :8, :], pltpu.roll(density[2 * j + 1, :8, :], 4, 0)
@@ -162,7 +157,6 @@
     on_packs(send_pack, lambda copy: copy.start(), False)
     on_rows(lines, lambda copy: copy.start())
 
-    on_packs(send_pack_d, lambda copy: copy.start(), False)
     on_rows(lines_d, lambda copy: copy.start())
 
     def send_weight(i, slot):
@@ -335,14 +329,13 @@
 
     lax.fori_loop(0, STEPS, diffuse, 0)
 
-    on_packs(send_pack_d, lambda copy: copy.wait_recv(), True)
     receive_rows(lines_d)
     upper = sub < 4
     for f in range(faces):
         turn = (lambda v: v) if f % 2 == 0 else (lambda v: pltpu.roll(v, 4, 0))
         whole = [strips[32 * f + 8 * e : 32 * f + 8 * e + 8, :] for e in range(4)]
         edge_rows = jnp.where(upper, turn(first_d[f // 2]), turn(last_d[f // 2]))
-        edge_columns = gather_strip(lambda s: packs_d[s], f)
+        edge_columns = gather_strip(lambda s: packs[s, 2], f)
         strips[16 * f : 16 * f + 8, :] = edge_rows / jnp.where(upper, whole[0], whole[1])
         strips[16 * f + 8 : 16 * f + 16, :] = edge_columns / jnp.where(upper, whole[2], whole[3])
         around = jnp.where(upper, turn(below_d[f // 2]), turn(above_d[f // 2]))
@@ -384,7 +377,6 @@
         send_logs(i, m).wait_send()
         send_weight(i, m).wait_send()
     on_packs(send_pack, lambda copy: copy.wait_send(), False)
-    on_packs(send_pack_d, lambda copy: copy.wait_send(), False)
     on_rows(lines, lambda copy: copy.wait_send())
     on_rows(lines_d, lambda copy: copy.wait_send())
     store_dual.wait()
@@ -427,17 +419,15 @@
             vmem(32, side),
             vmem(side + 16, LANES),
             vmem(3, faces, rows, side),
-            vmem(2, 8, LANES),
-            vmem(n, 2, 8, LANES),
+            vmem(3, 8, LANES),
+            vmem(n, 3, 8, LANES),
             *[vmem(faces, DEPTH, side)] * 4,
-            vmem(8, LANES),
-            vmem(n, 8, LANES),
             *[vmem(faces // 2, 8, side)] * 6,
             vmem(faces, rows, side),
             vmem(members, faces, rows, side),
             vmem(8, LANES),
             vmem(members, 8, LANES),
-            dma(5), dma(n), dma(n), dma(n), dma(n),
+            dma(5), dma(n), dma(n),
             dma(n + 1), dma(n + 1), dma(4), dma(n + 1), dma(n + 1), dma(4),
             dma(members), dma(members), dma(members), dma(members),
         ],

time: 20.7 us -> 20.8 us (level)
  no operation moved by 1% of the time
where the time goes in v7:
time: 20.8 us; the launch traced here: 20.6 us
  Pallas kernels  19.3 us (93%)
  between operations  1.29 us (6%)
    pallas_call x1, Pallas kernels, body(): pl.pallas_call(functools.partial(kernel, n, members, faces, rows, side),...  17.8 us
    pallas_call x1, Pallas kernels, body(): pl.pallas_call(hand_out, out_shape=(jax.ShapeDtypeStruct(scaling.shape, j...  1.52 us

profile of v7, /device:TPU:0, one launch (start us, length us, event | category | flops | bytes accessed | tf_op | source)
XLA Modules:
  0.0 20.6 jit_solution(15444891117805811651)
XLA Ops:
  1.3 17.8 %shard_map.67.results = f32[3,6,16,128]{3,2,1,0:T(8,128)} custom-call(s32[3,4,6]{2,1,0:T(4,128)} %seams_hbm.1, f32[1]{0:T(128)S(6)} %copy.7.weight_hbm, f32[1,6,16,128]{3,2,1,0:T(8,128)} %density_hbm.1, f32[1,6,16,128]{3,2,1,0:T(8,128)} %scaling_hbm.1), custom_call_target="tpu_custom_call" | custom-call | tf_op jit(solution)/shard_map/pallas_call | solution.py:407
  19.0 1.5 %shard_map.68 = (f32[1,6,16,128]{3,2,1,0:T(8,128)}, f32[1,6,16,128]{3,2,1,0:T(8,128)}, f32[6,16,128]{2,1,0:T(8,128)}) custom-call(f32[3,6,16,128]{3,2,1,0:T(8,128)} %shard_map.67.results), custom_call_target="tpu_custom_call" | custom-call | tf_op jit(solution)/shard_map/pallas_call | solution.py:438

commit v8 on v7

--- a/solution.py
+++ b/solution.py
@@ -327,7 +327,7 @@
                 tile[f, 8 * j + 8 : 8 * j + 16, :] = value
         return carry
 
-    lax.fori_loop(0, STEPS, diffuse, 0)
+    lax.fori_loop(0, STEPS, diffuse, 0, unroll=2)
 
     receive_rows(lines_d)
     upper = sub < 4
@@ -345,7 +345,7 @@
         results[1, f] = dual
     store_dual = pltpu.make_async_copy(results.at[1], out_hbm.at[1], local.at[2])
     store_dual.start()
-    lax.fori_loop(0, STEPS, diffuse_merged, 0)
+    lax.fori_loop(0, STEPS, diffuse_merged, 0, unroll=2)
 
     marginal = scaling[...] * tile[:, 8 : 8 + rows, :]
     logs[...] = weight_ref[0] * jnp.log(marginal)

time: 20.8 us -> 20.7 us (level)
  no operation moved by 1% of the time
where the time goes in v8:
time: 20.7 us; the launch traced here: 20.5 us
  Pallas kernels  19.2 us (93%)
  between operations  1.29 us (6%)
    pallas_call x1, Pallas kernels, body(): pl.pallas_call(functools.partial(kernel, n, members, faces, rows, side),...  17.7 us
    pallas_call x1, Pallas kernels, body(): pl.pallas_call(hand_out, out_shape=(jax.ShapeDtypeStruct(scaling.shape, j...  1.52 us

profile of v8, /device:TPU:0, one launch (start us, length us, event | category | flops | bytes accessed | tf_op | source)
XLA Modules:
  0.0 20.5 jit_solution(6415939803432612975)
XLA Ops:
  1.3 17.7 %shard_map.67.results = f32[3,6,16,128]{3,2,1,0:T(8,128)} custom-call(s32[3,4,6]{2,1,0:T(4,128)} %seams_hbm.1, f32[1]{0:T(128)S(6)} %copy.7.weight_hbm, f32[1,6,16,128]{3,2,1,0:T(8,128)} %density_hbm.1, f32[1,6,16,128]{3,2,1,0:T(8,128)} %scaling_hbm.1), custom_call_target="tpu_custom_call" | custom-call | tf_op jit(solution)/shard_map/pallas_call | solution.py:407
  19.0 1.5 %shard_map.68 = (f32[1,6,16,128]{3,2,1,0:T(8,128)}, f32[1,6,16,128]{3,2,1,0:T(8,128)}, f32[6,16,128]{2,1,0:T(8,128)}) custom-call(f32[3,6,16,128]{3,2,1,0:T(8,128)} %shard_map.67.results), custom_call_target="tpu_custom_call" | custom-call | tf_op jit(solution)/shard_map/pallas_call | solution.py:438
